TPU v7x, 512 devices: a whole 4x4x16 slice. The times are simulated.
512 devices in a mesh: lag: 8 (over x_hi, y), col: 64 (over z, x_lo, core).
Axes of the slice: x: 4 (x_hi: 2, x_lo: 2; x = x_hi * 2 + x_lo), y: 4, z: 16, core: 2. Of those that a mesh axis runs over, the one named last changes fastest.
Arguments:
- background: bfloat16 [8, 512, 6, 64, 128], P('lag', 'col'), may hold values from -16 to 16
- obs_ensemble: bfloat16 [8, 512, 128, 128], P('lag', 'col'), may hold values from -12 to 12
- obs_value: bfloat16 [8, 512, 128], P('lag', 'col'), may hold values from -12 to 12
- obs_weight: bfloat16 [8, 512, 128], P('lag', 'col'), may hold values from 0.099609375 to 1
- obs_count: int32 [8, 512], P('lag', 'col'), may hold values from 32 to 128, as said below
Outputs:
- analysis: bfloat16 [8, 512, 6, 64, 128], P('lag', 'col')
Inputs may be any that keep to these rules, and one draw needn't show every extreme that they name: `obs_count`: each slot has at least one patch with exactly 128 live observations.
All inputs are finite; a program needn't handle non-finite values.
Results may differ from a plain program's by a relative error of at most 0.006.
Values may be sent and summed in bfloat16 or wider, within the bound.
No kernel may reach another device: no remote copies, remote signals or barrier semaphores. Data moves between devices by JAX's collectives and lax.ppermute only.
A program may use at most 64 MiB of HBM per device.

v0:
```python
import jax
import jax.numpy as jnp
from jax import lax
from jax.sharding import PartitionSpec as P

ITERS = 12
REACH = 4


relaxation = 0.9
epsilon = 1e-06


def with_halo(block, sides, width):
    for axis, dim in sides:
        count = lax.axis_size(axis)
        forward = [(i, i + 1) for i in range(count - 1)]
        forward.append((count - 1, 0))
        backward = [(target, source) for source, target in forward]
        low = lax.ppermute(
            lax.slice_in_dim(block, block.shape[dim] - width, None, axis=dim), axis, forward
        )
        high = lax.ppermute(lax.slice_in_dim(block, 0, width, axis=dim), axis, backward)
        block = jnp.concatenate([low, block, high], axis=dim)
    return block


def slot_terms(obs_ensemble, obs_value, weight):
    ensemble = obs_ensemble.astype(jnp.float32)
    center = jnp.mean(ensemble, axis=-1, keepdims=True)
    spread = ensemble - center
    innovation = obs_value.astype(jnp.float32) - center[..., 0]
    scaled = spread * weight.astype(jnp.float32)[..., None]
    gram_sum = jnp.einsum("spok,spol->pkl", spread, scaled, precision=lax.Precision.HIGHEST)
    vector_sum = jnp.einsum("spok,spo->pk", scaled, innovation, precision=lax.Precision.HIGHEST)
    return jnp.concatenate([gram_sum, vector_sum[:, None, :]], axis=1)


def localize(system):
    local_count = system.shape[0]
    padded = with_halo(system, (("col", 0),), REACH)
    total = padded[REACH : REACH + local_count]
    for offset in range(1, REACH + 1):
        taper_weight = 1.0 - offset / (REACH + 1.0)
        before = padded[REACH - offset : REACH - offset + local_count]
        after = padded[REACH + offset : REACH + offset + local_count]
        total = total + taper_weight * (before + after)
    return total


def square_roots(system):
    grams = system[:, :-1, :]
    vectors = system[:, -1, :]
    members = grams.shape[-1]
    identity = jnp.eye(members, dtype=jnp.float32)
    matrix = grams + (members - 1.0) * identity
    norm_bound = jnp.sum(jnp.abs(matrix), axis=(1, 2))
    root_est = matrix / norm_bound[:, None, None]
    inverse_root = jnp.broadcast_to(identity, matrix.shape)
    for sweep in range(ITERS):
        middle = 1.5 * identity - 0.5 * jnp.einsum(
            "pij,pjk->pik", inverse_root, root_est, precision=lax.Precision.HIGHEST
        )
        root_est = jnp.einsum("pij,pjk->pik", root_est, middle, precision=lax.Precision.HIGHEST)
        inverse_root = jnp.einsum(
            "pij,pjk->pik", middle, inverse_root, precision=lax.Precision.HIGHEST
        )
    scale_root = jnp.sqrt((members - 1.0) / norm_bound)
    inner_prod = jnp.einsum("pij,pj->pi", inverse_root, vectors, precision=lax.Precision.HIGHEST)
    mean_weight = (
        jnp.einsum("pij,pj->pi", inverse_root, inner_prod, precision=lax.Precision.HIGHEST)
        / norm_bound[:, None]
    )
    mixing = inverse_root * scale_root[:, None, None] + mean_weight[:, :, None]
    return mixing.astype(jnp.bfloat16)


def apply_weights(prior_spread, mixing):
    return jnp.einsum("plck,pkj->plcj", prior_spread, mixing, preferred_element_type=jnp.float32)


def shards(background, obs_ensemble, obs_value, obs_weight, obs_count):
    members = background.shape[-1]
    local_patches = background.shape[1]
    columns = background.shape[3]
    live_slots = lax.broadcasted_iota(jnp.int32, obs_value.shape, 2) < obs_count[:, :, None]
    weight = jnp.where(live_slots, obs_weight, jnp.zeros_like(obs_weight))
    states = background[0].astype(jnp.float32)
    prior_center = jnp.mean(states, axis=-1, keepdims=True)
    prior_spread = (states - prior_center).astype(jnp.bfloat16)
    prior_square = jnp.sum(jnp.square(prior_spread.astype(jnp.float32)), axis=(0, 2, 3))
    prior_total = lax.psum(prior_square, "col")
    system = localize(slot_terms(obs_ensemble, obs_value, weight))
    summed = lax.psum(system, "lag")
    mixing = square_roots(summed)
    increment = apply_weights(prior_spread, mixing)
    posterior = prior_center + increment
    post_center = jnp.mean(posterior, axis=-1, keepdims=True)
    post_spread = posterior - post_center
    post_square = jnp.sum(jnp.square(post_spread), axis=(0, 2, 3))
    post_total = lax.psum(post_square, "col")
    divisor = (members - 1.0) * local_patches * lax.axis_size("col") * columns
    prior_sd = jnp.sqrt(prior_total / divisor + epsilon)
    post_sd = jnp.sqrt(post_total / divisor + epsilon)
    factor = 1.0 + relaxation * (prior_sd - post_sd) / post_sd
    result = post_center + factor[None, :, None, None] * post_spread
    return result.astype(jnp.bfloat16)[None]


def solution(mesh):
    placed = (
        P("lag", "col", None, None, None),
        P("lag", "col", None, None),
        P("lag", "col", None),
        P("lag", "col", None),
        P("lag", "col"),
    )
    return jax.shard_map(
        shards,
        mesh=mesh,
        in_specs=placed,
        out_specs=P("lag", "col", None, None, None),
        check_vma=False,
    )
```

profile of v0, /device:TPU:1, one launch (start us, length us, event | category | flops | bytes accessed | tf_op | source)
XLA Modules:
  0.0 277.3 jit_solution(6325371914765706938)
XLA Ops:
  6.5 1.2 convert_reduce_fusion.1
  7.7 0.7 bitcast_subtract_fusion
  8.4 0.8 fusion.51
  9.2 2.5 fusion.26
  11.7 1.7 fusion.29
  13.5 4.5 %collective-permute-start = (f32[4,129,128]{2,1,0:T(8,128)S(1)}, f32[4,129,128]{2,1,0:T(8,128)S(1)}, u32[]{:S(2)}, u32[]{:S(2)}) collective-permute-start(f32[4,129,128]{2,1,0:T(8,128)S(1)} %get-tuple-element.9), channel_id=1, source_target_pairs={{0,1},{1,2},{2,3},{3,4},{4,5},{5,6},{6,7},{7,8},{8,9},{9,10},{10,1... | collective-permute-start | bytes 792584 | tf_op jit(solution)/shard_map/ppermute | solution.py:20
  18.0 6.4 %collective-permute-start.1 = (f32[4,129,128]{2,1,0:T(8,128)S(1)}, f32[4,129,128]{2,1,0:T(8,128)S(1)}, u32[]{:S(2)}, u32[]{:S(2)}) collective-permute-start(f32[4,129,128]{2,1,0:T(8,128)S(1)} %get-tuple-element.10), channel_id=1, source_target_pairs={{1,0},{2,1},{3,2},{4,3},{5,4},{6,5},{7,6},{8,7},{9,8},{10,9},{11,1... | collective-permute-start | bytes 792584 | tf_op jit(solution)/shard_map/ppermute | solution.py:23
  24.9 1.0 collective-permute-done.1
  26.0 1.0 fusion.21
  27.6 100.6 %all-reduce.3.cloned.1.call-done = f32[8,129,128]{2,1,0:T(8,128)} async-done(((f32[8,129,128]{2,1,0:T(8,128)}), f32[8,129,128]{2,1,0:T(8,128)}) %all-reduce.3.cloned.1.call-update) | async-done | bytes 528400 | tf_op jit(solution)/shard_map/psum | solution.py:94
  128.3 1.2 abs_reduce_fusion
  129.5 1.8 fusion.13
  131.9 0.7 fusion.53
  132.6 0.6 fusion.12
  138.5 0.6 fusion.9
  140.4 0.9 fusion.8
  144.6 0.6 fusion.6
  150.5 0.6 fusion.3
  152.5 0.9 fusion.2
  154.1 0.9 convolution_bitcast_fusion
  155.0 0.9 fusion.78
  156.0 2.1 fusion.56
  158.6 110.5 %all-reduce = (f32[6]{0:T(128)S(1)}, f32[6]{0:T(128)S(1)}) all-reduce(f32[6]{0:T(128)S(1)} %multiply_reduce_fusion, f32[6]{0:T(128)S(1)} %multiply_reduce_fusion.1), channel_id=1, replica_groups=mesh['lag'=8,'col'=64] {'col'}, use_global_device_ids=true, to_apply=%region_8.9 | all-reduce | flops 12 | bytes 96 | tf_op jit(solution)/shard_map/psum | solution.py:101
  269.1 1.4 fusion.14
  (47 shorter events, 19.3 us)
Async XLA Ops:
  6.5 17.8 %copy-start = (bf16[1,8,6,64,128]{4,3,2,1,0:T(8,128)(2,1)S(1)}, bf16[1,8,6,64,128]{4,3,2,1,0:T(8,128)(2,1)}, u32[]{:S(2)}) copy-start(bf16[1,8,6,64,128]{4,3,2,1,0:T(8,128)(2,1)} %param.5) | copy-start | bytes 2359300
  6.5 121.7 %all-reduce.3.cloned.1.call-start = ((), (), s32[]{:S(2)}) async-start(), calls=%async_computation | async-start | bytes 1114112 | tf_op jit(solution)/shard_map/psum | solution.py:94
  13.5 11.4 %collective-permute-start = (f32[4,129,128]{2,1,0:T(8,128)S(1)}, f32[4,129,128]{2,1,0:T(8,128)S(1)}, u32[]{:S(2)}, u32[]{:S(2)}) collective-permute-start(f32[4,129,128]{2,1,0:T(8,128)S(1)} %get-tuple-element.9), channel_id=1, source_target_pairs={{0,1},{1,2},{2,3},{3,4},{4,5},{5,6},{6,7},{7,8},{8,9},{9,10},{10,1... | collective-permute-start | bytes 792584 | tf_op jit(solution)/shard_map/ppermute | solution.py:20
  18.0 7.9 %collective-permute-start.1 = (f32[4,129,128]{2,1,0:T(8,128)S(1)}, f32[4,129,128]{2,1,0:T(8,128)S(1)}, u32[]{:S(2)}, u32[]{:S(2)}) collective-permute-start(f32[4,129,128]{2,1,0:T(8,128)S(1)} %get-tuple-element.10), channel_id=1, source_target_pairs={{1,0},{2,1},{3,2},{4,3},{5,4},{6,5},{7,6},{8,7},{9,8},{10,9},{11,1... | collective-permute-start | bytes 792584 | tf_op jit(solution)/shard_map/ppermute | solution.py:23
  129.5 2.4 copy-start.1
Sparse Core Ops, SparseCore 0:
  27.2 101.0 all-reduce.2
where the time goes:
time: 278 us; the launch traced here: 277 us
  blocking collectives  110 us (40%)
  waiting for transfers between devices  102 us (37%)
  matrix products  32.5 us (12%)
  between operations  13.8 us (5%)
  starting transfers between devices  10.9 us (4%)
  other arithmetic  8.12 us (3%)
    psum x1, blocking collectives, shards(): post_total = lax.psum(post_square, 'col')  110 us
    psum x1, waiting for transfers between devices, shards(): summed = lax.psum(system, 'lag')  101 us
    dot_general x12, matrix products, square_roots(): jnp.einsum('pij,pjk->pik', inverse_root, root_est, precision=lax.Precisio...  9.42 us
    dot_general x12, matrix products, square_roots(): jnp.einsum('pij,pjk->pik', middle, inverse_root, precision=lax.Precision....  7.7 us
    dot_general x11, matrix products, square_roots(): jnp.einsum('pij,pjk->pik', root_est, middle, precision=lax.Precision.HIGH...  7.17 us
    ppermute x1, starting transfers between devices, with_halo(): lax.ppermute(lax.slice_in_dim(block, 0, width, axis=dim), axis, backward)  6.38 us
  transfers between devices with their start and end apart: 3, of which 2 were waited for; matrix products, arithmetic and copies ran while one was open for 0% of the time, Pallas kernels for 0%

commit v1 on v0

v1 whole, which is shorter than its diff:
```python
import jax
import jax.numpy as jnp
from jax import lax
from jax.experimental import pallas as pl
from jax.experimental.pallas import tpu as pltpu
from jax.sharding import PartitionSpec as P

ITERS = 12
REACH = 4
RELAXATION = 0.9
EPSILON = 1e-06
MEMBERS = 128
HALF = MEMBERS // 2
PACKED = 72

bf16 = jnp.bfloat16
f32 = jnp.float32


def iota2(shape, dim):
    return lax.broadcasted_iota(jnp.int32, shape, dim)


def halves(value):
    high = value.astype(bf16)
    return high, (value - high.astype(f32)).astype(bf16)


def dot(left, right):
    return jnp.dot(left, right, preferred_element_type=f32)


def pack(gram, vector):
    row, lane = iota2((HALF, MEMBERS), 0), iota2((HALF, MEMBERS), 1)
    lower = pltpu.roll(gram[HALF:], HALF, 1)
    matrix = jnp.where(lane >= row, gram[:HALF], lower)
    diagonal = jnp.sum(jnp.where(lane == row, lower, 0.0), axis=0, keepdims=True)
    tail = iota2((8, MEMBERS), 0)
    rest = jnp.where(tail == 0, diagonal, jnp.where(tail == 1, vector, 0.0))
    return jnp.concatenate([matrix, rest], axis=0)


def unpack(packed):
    row, lane = iota2((HALF, MEMBERS), 0), iota2((HALF, MEMBERS), 1)
    matrix = packed[:HALF]
    diagonal = packed[HALF : HALF + 1]
    vector = packed[HALF + 1 : HALF + 2]
    flipped = jnp.transpose(jnp.concatenate([matrix, jnp.zeros_like(matrix)], axis=0))
    upper = jnp.where(lane >= row, matrix, flipped[:HALF])
    corner = jnp.where(lane == row, diagonal, jnp.where(lane < row, matrix, flipped[:HALF]))
    lower = jnp.where(lane < HALF, flipped[HALF:], pltpu.roll(corner, HALF, 1))
    return jnp.concatenate([upper, lower], axis=0), vector


def statistics_kernel(count_ref, ensemble_ref, value_ref, weight_ref, out_ref, system_ref):
    patches = ensemble_ref.shape[0]
    lane = iota2((1, MEMBERS), 1)
    for p in range(patches):
        ensemble = ensemble_ref[p]
        weight = weight_ref[p : p + 1, :].astype(f32)
        weight = jnp.where(lane < count_ref[p], weight, 0.0)
        weighted_value = weight * value_ref[p : p + 1, :].astype(f32)
        flipped = jnp.transpose(ensemble.astype(f32)) * weight
        rows = jnp.concatenate(
            [flipped, jnp.broadcast_to(weighted_value, (16, MEMBERS))], axis=0
        )
        high, low = halves(rows)
        sums = dot(
            jnp.concatenate([high, low], axis=1), jnp.concatenate([ensemble, ensemble], axis=0)
        )
        system_ref[p] = pack(sums[:MEMBERS], sums[MEMBERS : MEMBERS + 1])
    for target in range(-REACH, patches + REACH):
        total = None
        for p in range(patches):
            distance = abs(target - p)
            if distance <= REACH:
                term = (1.0 - distance / (REACH + 1.0)) * system_ref[p]
                total = term if total is None else total + term
        if 0 <= target < patches:
            out_ref[target, 0] = total
        else:
            out_ref[target % patches, 1] = total


def statistics(obs_count, obs_ensemble, obs_value, obs_weight):
    patches = obs_ensemble.shape[0]
    vmem = pl.BlockSpec(memory_space=pltpu.VMEM)
    return pl.pallas_call(
        statistics_kernel,
        out_shape=jax.ShapeDtypeStruct((patches, 2, PACKED, MEMBERS), f32),
        in_specs=[pl.BlockSpec(memory_space=pltpu.SMEM), vmem, vmem, vmem],
        out_specs=vmem,
        scratch_shapes=[pltpu.VMEM((patches, PACKED, MEMBERS), f32)],
        compiler_params=pltpu.CompilerParams(vmem_limit_bytes=16 * 1024 * 1024),
    )(obs_count, obs_ensemble, obs_value, obs_weight)


def solver_kernel(received_ref, beside_ref, out_ref):
    total = beside_ref[...]
    for s in range(received_ref.shape[0]):
        total = total + received_ref[s, 0]
    gram, vector = unpack(total)
    scale = 1.0 / MEMBERS
    mean_row = jnp.sum(gram, axis=0, keepdims=True) * scale
    mean_column = jnp.sum(gram, axis=1, keepdims=True) * scale
    mean_all = jnp.sum(mean_row, axis=1, keepdims=True) * scale
    vector = vector - mean_row
    vector = vector - jnp.sum(vector, axis=1, keepdims=True) * scale
    shape = (MEMBERS, MEMBERS)
    identity = jnp.where(iota2(shape, 0) == iota2(shape, 1), 1.0, 0.0)
    matrix = gram - mean_row - mean_column + mean_all + (MEMBERS - 1.0) * identity
    bound = jnp.sum(jnp.sum(jnp.abs(matrix), axis=0, keepdims=True), axis=1, keepdims=True)
    state = matrix / bound
    inverse_root = None
    for sweep in range(ITERS):
        middle = 1.5 * identity - 0.5 * state
        high, low = halves(middle)
        right = jnp.concatenate(
            [jnp.concatenate([high, low], axis=1), jnp.concatenate([low, high], axis=1)], axis=0
        )

        def times_middle(left):
            product = dot(jnp.concatenate(halves(left), axis=1), right)
            return product[:, :MEMBERS] + product[:, MEMBERS:]

        if sweep < ITERS - 1:
            state = times_middle(times_middle(state))
        inverse_root = middle if sweep == 0 else times_middle(inverse_root)
    inner = jnp.sum(inverse_root * vector, axis=1, keepdims=True)
    mean_weight = jnp.sum(inverse_root * inner, axis=0, keepdims=True) / bound
    mean_weight = jnp.sum(jnp.where(identity > 0.0, mean_weight, 0.0), axis=1, keepdims=True)
    mixing = inverse_root * jnp.sqrt((MEMBERS - 1.0) / bound) + mean_weight
    out_ref[...] = jnp.broadcast_to(mixing.astype(bf16)[None], out_ref.shape)


def solver(received, beside):
    vmem = pl.BlockSpec(memory_space=pltpu.VMEM)
    return pl.pallas_call(
        solver_kernel,
        out_shape=jax.ShapeDtypeStruct((received.shape[0], MEMBERS, MEMBERS), bf16),
        in_specs=[vmem, vmem],
        out_specs=vmem,
        compiler_params=pltpu.CompilerParams(vmem_limit_bytes=16 * 1024 * 1024),
    )(received, beside)


def apply_kernel(states_ref, mixing_ref, spread_ref, center_ref, sums_ref, square_ref):
    p = pl.program_id(0)
    levels, columns = states_ref.shape[1], states_ref.shape[2]
    rows = levels * columns

    @pl.when(p == 0)
    def _():
        square_ref[...] = jnp.zeros_like(square_ref)

    states = states_ref[0].reshape(rows, MEMBERS)
    average = jnp.full((MEMBERS, MEMBERS), 1.0 / MEMBERS, bf16)
    prior_center = dot(states, average)
    prior_spread = (states.astype(f32) - prior_center).astype(bf16)
    mixing = mixing_ref[0].astype(f32)
    mixing_center = jnp.sum(mixing, axis=1, keepdims=True) * (1.0 / MEMBERS)
    spread_high, spread_low = halves(mixing - mixing_center)
    center_high, center_low = halves(jnp.broadcast_to(mixing_center, mixing.shape))
    right = jnp.concatenate(
        [
            jnp.concatenate([spread_high, center_high], axis=1),
            jnp.concatenate([spread_low, center_low], axis=1),
        ],
        axis=0,
    )
    product = dot(jnp.concatenate([prior_spread, prior_spread], axis=1), right)
    post_spread = product[:, :MEMBERS]
    spread_ref[0] = post_spread.reshape(levels, columns, MEMBERS)
    center_ref[0] = (prior_center + product[:, MEMBERS:]).reshape(levels, columns, MEMBERS)
    prior_square = jnp.square(prior_spread.astype(f32)).reshape(levels, columns // 8, 8, MEMBERS)
    post_square = jnp.square(post_spread).reshape(levels, columns // 8, 8, MEMBERS)
    square_ref[0] += jnp.sum(prior_square, axis=1)
    square_ref[1] += jnp.sum(post_square, axis=1)

    @pl.when(p == pl.num_programs(0) - 1)
    def _():
        sums = jnp.sum(square_ref[...], axis=2).reshape(2 * levels, MEMBERS)
        sums = jnp.concatenate(
            [sums, jnp.zeros((MEMBERS - 2 * levels, MEMBERS), f32)], axis=0
        )
        sums = jnp.sum(jnp.transpose(sums), axis=0, keepdims=True)
        sums_ref[...] = jnp.broadcast_to(sums, sums_ref.shape)


def apply_weights(states, mixing, receivers):
    patches, levels, columns, members = states.shape
    block = pl.BlockSpec((1, levels, columns, members), lambda p: (p, 0, 0, 0))
    return pl.pallas_call(
        apply_kernel,
        grid=(patches,),
        out_shape=(
            jax.ShapeDtypeStruct(states.shape, f32),
            jax.ShapeDtypeStruct(states.shape, f32),
            jax.ShapeDtypeStruct((receivers, members), f32),
        ),
        in_specs=[block, pl.BlockSpec((1, members, members), lambda p: (p, 0, 0))],
        out_specs=(block, block, pl.BlockSpec((receivers, members), lambda p: (0, 0))),
        scratch_shapes=[pltpu.VMEM((2, levels, 8, members), f32)],
        compiler_params=pltpu.CompilerParams(vmem_limit_bytes=16 * 1024 * 1024),
    )(states, mixing)


def finish_kernel(divisor, sums_ref, spread_ref, center_ref, out_ref):
    levels = spread_ref.shape[1]
    sums = jnp.sum(sums_ref[...], axis=0, keepdims=True)
    deviation = jnp.sqrt(sums / divisor + EPSILON)
    lane = iota2(deviation.shape, 1)
    for level in range(levels):
        prior_sd = jnp.sum(jnp.where(lane == level, deviation, 0.0), axis=1, keepdims=True)
        post_sd = jnp.sum(jnp.where(lane == levels + level, deviation, 0.0), axis=1, keepdims=True)
        factor = 1.0 + RELAXATION * (prior_sd - post_sd) / post_sd
        out_ref[0, level] = (center_ref[0, level] + factor * spread_ref[0, level]).astype(bf16)


def finish(sums, spread, center, divisor):
    patches, levels, columns, members = spread.shape
    block = pl.BlockSpec((1, levels, columns, members), lambda p: (p, 0, 0, 0))

    def kernel(*refs):
        finish_kernel(divisor, *refs)

    return pl.pallas_call(
        kernel,
        grid=(patches,),
        out_shape=jax.ShapeDtypeStruct(spread.shape, bf16),
        in_specs=[pl.BlockSpec(sums.shape, lambda p: (0, 0)), block, block],
        out_specs=block,
        compiler_params=pltpu.CompilerParams(vmem_limit_bytes=16 * 1024 * 1024),
    )(sums, spread, center)


def shards(background, obs_ensemble, obs_value, obs_weight, obs_count):
    lags, tiles = lax.axis_size("lag"), lax.axis_size("col")
    patches, columns = background.shape[1], background.shape[3]
    sent = statistics(obs_count[0], obs_ensemble[0], obs_value[0], obs_weight[0])
    received = lax.all_to_all(sent, "lag", 0, 0)
    beside = jnp.sum(received[:, 1], axis=0)
    moves = [
        (i * tiles + c, i * tiles + (c + (1 if i < REACH else -1)) % tiles)
        for i in range(lags)
        for c in range(tiles)
    ]
    beside = lax.ppermute(beside, ("lag", "col"), moves)
    mixing = lax.all_to_all(solver(received, beside), "lag", 0, 0)
    spread, center, sums = apply_weights(background[0], mixing, tiles)
    sums = lax.all_to_all(sums, "col", 0, 0, tiled=True)
    divisor = (MEMBERS - 1.0) * patches * tiles * columns
    return finish(sums, spread, center, divisor)[None]


def solution(mesh):
    placed = (
        P("lag", "col", None, None, None),
        P("lag", "col", None, None),
        P("lag", "col", None),
        P("lag", "col", None),
        P("lag", "col"),
    )
    return jax.shard_map(
        shards,
        mesh=mesh,
        in_specs=placed,
        out_specs=P("lag", "col", None, None, None),
        check_vma=False,
    )
```

time: 278 us -> 82.5 us (0.30)
  waiting for transfers between devices: 102 us -> 1.04 us
  blocking collectives: 110 us -> 61.7 us
  matrix products: 32.5 us -> 0 us
  between operations: 13.8 us -> 0.05 us
  Pallas kernels: 0 us -> 11.2 us
  other arithmetic: 8.12 us -> 0.02 us
  starting transfers between devices: 10.9 us -> 5.19 us
  local copies, waits for them, and re-layouts: 0.01 us -> 2.97 us
    psum x1 -> x0, blocking collectives: 110 us -> none  [shards(): post_total = lax.psum(post_square, 'col')]
    psum x1 -> x0, waiting for transfers between devices: 101 us -> none  [shards(): summed = lax.psum(system, 'lag')]
    all_to_all x0 -> x3, blocking collectives: none -> 61.7 us  [the longest x1 33.1 us: shards(): sums = lax.all_to_all(sums, 'col', 0, 0, tiled=True)]
    dot_general x40 -> x0, matrix products: 32.5 us -> none  [the longest x12 9.42 us: square_roots(): jnp.einsum('pij,pjk->pik', inverse_root, root_est, precision=lax.Precisio...]
    pallas_call x0 -> x4, Pallas kernels: none -> 11.2 us  [the longest x1 4 us: solver(): pl.pallas_call(solver_kernel, out_shape=jax.ShapeDtypeStruct((received.sh...]
    ppermute x2 -> x1, starting transfers between devices: 10.9 us -> 5.19 us  [shards(): beside = lax.ppermute(beside, ('lag', 'col'), moves)]
    reduce_sum x5 -> x1, other arithmetic: 3.97 us -> 0.02 us  [shards(): beside = jnp.sum(received[:, 1], axis=0)]
    unnamed x4 -> x10, local copies, waits for them, and re-layouts: 0.01 us -> 2.97 us
  transfers between devices with their start and end apart: 3 -> 1, of which waited for: 2 -> 1; matrix products, arithmetic and copies ran while one was open for 0% -> 0% of each run, Pallas kernels for 0% -> 0%
where the time goes in v1:
time: 82.5 us; the launch traced here: 82.2 us
  blocking collectives  61.7 us (75%)
  Pallas kernels  11.2 us (14%)
  starting transfers between devices  5.19 us (6%)
  local copies, waits for them, and re-layouts  2.97 us (4%)
  waiting for transfers between devices  1.04 us (1%)
    all_to_all x1, blocking collectives, shards(): sums = lax.all_to_all(sums, 'col', 0, 0, tiled=True)  33.1 us
    all_to_all x1, blocking collectives, shards(): received = lax.all_to_all(sent, 'lag', 0, 0)  17.7 us
    all_to_all x1, blocking collectives, shards(): mixing = lax.all_to_all(solver(received, beside), 'lag', 0, 0)  10.9 us
    ppermute x1, starting transfers between devices, shards(): beside = lax.ppermute(beside, ('lag', 'col'), moves)  5.19 us
    pallas_call x1, Pallas kernels, solver(): pl.pallas_call(solver_kernel, out_shape=jax.ShapeDtypeStruct((received.sh...  4 us
    pallas_call x1, Pallas kernels, finish(): pl.pallas_call(kernel, grid=(patches,), out_shape=jax.ShapeDtypeStruct(sp...  3.22 us
    unnamed x10, local copies, waits for them, and re-layouts  2.97 us
    pallas_call x1, Pallas kernels, apply_weights(): pl.pallas_call(apply_kernel, grid=(patches,), out_shape=(jax.ShapeDtypeSt...  2.95 us
  transfers between devices with their start and end apart: 1, of which 1 were waited for; matrix products, arithmetic and copies ran while one was open for 0% of the time, Pallas kernels for 0%

profile of v1, /device:TPU:1, one launch (start us, length us, event | category | flops | bytes accessed | tf_op | source)
XLA Modules:
  0.0 82.2 jit_solution(9875638674820060891)
XLA Ops:
  0.0 0.0 copy-start.1
  0.0 0.9 %copy-done.1 = bf16[1,8,128,128]{3,2,1,0:T(8,128)(2,1)S(1)} copy-done((bf16[1,8,128,128]{3,2,1,0:T(8,128)(2,1)S(1)}, bf16[1,8,128,128]{3,2,1,0:T(8,128)(2,1)}, u32[]{:S(2)}) %copy-start.1) | copy-done | bytes 262168
  1.0 0.0 copy-start.2
  1.0 0.7 copy-done.2
  1.6 0.0 copy-start.3
  1.6 0.7 copy-done.3
  2.3 0.0 copy-start.4
  2.3 0.7 copy-done.4
  3.0 1.0 %shard_map.55 = f32[8,2,72,128]{3,2,1,0:T(8,128)S(1)} custom-call(s32[8]{0:T(128)S(1)} %bitcast.16, bf16[8,128,128]{2,1,0:T(8,128)(2,1)S(1)} %bitcast.11, bf16[8,128]{1,0:T(8,128)(2,1)S(1)} %bitcast.14, bf16[8,128]{1,0:T(8,128)(2,1)S(1)} %bitcast.15), custom_call_target="tpu_custom_call" | custom-call | tf_op jit(solution)/shard_map/pallas_call | solution.py:88
  4.0 0.0 copy-start
  4.0 17.7 %all_to_all.21.received_ref = f32[8,2,72,128]{3,2,1,0:T(8,128)S(1)} all-to-all(f32[8,2,72,128]{3,2,1,0:T(8,128)S(1)} %shard_map.55), channel_id=1, replica_groups=mesh['lag'=8,'col'=64] {'lag'}, dimensions={0} | all-to-all | bytes 1179648 | tf_op jit(solution)/shard_map/all_to_all | solution.py:241
  21.7 5.2 %collective-permute-start = (f32[72,128]{1,0:T(8,128)S(1)}, f32[72,128]{1,0:T(8,128)S(1)}, u32[]{:S(2)}, u32[]{:S(2)}) collective-permute-start(f32[72,128]{1,0:T(8,128)S(1)} %slice_reduce_fusion), channel_id=1, source_target_pairs={{0,1},{1,2},{2,3},{3,4},{4,5},{5,6},{6,7},{7,8},{8,9},{9,10},{10,1... | collective-permute-start | bytes 110600 | tf_op jit(solution)/shard_map/ppermute | solution.py:248
  26.9 1.0 %collective-permute-done.beside_ref = f32[72,128]{1,0:T(8,128)S(1)} collective-permute-done((f32[72,128]{1,0:T(8,128)S(1)}, f32[72,128]{1,0:T(8,128)S(1)}, u32[]{:S(2)}, u32[]{:S(2)}) %collective-permute-start) | collective-permute-done | bytes 36896 | tf_op jit(solution)/shard_map/ppermute | solution.py:248
  28.0 4.0 %shard_map.56 = bf16[8,128,128]{2,1,0:T(8,128)(2,1)S(1)} custom-call(f32[8,2,72,128]{3,2,1,0:T(8,128)S(1)} %all_to_all.21.received_ref, f32[72,128]{1,0:T(8,128)S(1)} %collective-permute-done.beside_ref), custom_call_target="tpu_custom_call" | custom-call | tf_op jit(solution)/shard_map/pallas_call | solution.py:138
  32.0 10.9 %all_to_all.22.mixing_ref = bf16[8,128,128]{2,1,0:T(8,128)(2,1)S(1)} all-to-all(bf16[8,128,128]{2,1,0:T(8,128)(2,1)S(1)} %shard_map.56), channel_id=1, replica_groups=mesh['lag'=8,'col'=64] {'lag'}, dimensions={0} | all-to-all | bytes 524288 | tf_op jit(solution)/shard_map/all_to_all | solution.py:249
  42.9 0.0 copy-done
  42.9 3.0 %shard_map.57 = (f32[8,6,64,128]{3,2,1,0:T(8,128)S(1)}, f32[8,6,64,128]{3,2,1,0:T(8,128)S(1)}, f32[64,128]{1,0:T(8,128)S(1)}) custom-call(bf16[8,6,64,128]{3,2,1,0:T(8,128)(2,1)S(1)} %bitcast.10, bf16[8,128,128]{2,1,0:T(8,128)(2,1)S(1)} %all_to_all.22.mixing_ref), custom_call_target="tpu_custom_call" | custom-call | tf_op jit(solution)/shard_map/pallas_call | solution.py:193
  45.8 33.1 %all_to_all.23 = f32[64,1,128]{2,1,0:T(1,128)S(1)} all-to-all(f32[64,1,128]{2,1,0:T(1,128)S(1)} %bitcast.13), channel_id=1, replica_groups=mesh['lag'=8,'col'=64] {'col'}, dimensions={0} | all-to-all | bytes 65536 | tf_op jit(solution)/shard_map/all_to_all | solution.py:251
  79.0 3.2 %shard_map.58 = bf16[8,6,64,128]{3,2,1,0:T(8,128)(2,1)} custom-call(f32[64,128]{1,0:T(8,128)S(1)} %bitcast.12, f32[8,6,64,128]{3,2,1,0:T(8,128)S(1)} %get-tuple-element.9.refs_1_, f32[8,6,64,128]{3,2,1,0:T(8,128)S(1)} %get-tuple-element.10.refs_2_), custom_call_target="tpu_custom_call" | custom-call | tf_op jit(solution)/shard_map/pallas_call | solution.py:227
  (1 shorter events, 0.0 us)
Async XLA Ops:
  0.0 0.9 %copy-start.1 = (bf16[1,8,128,128]{3,2,1,0:T(8,128)(2,1)S(1)}, bf16[1,8,128,128]{3,2,1,0:T(8,128)(2,1)}, u32[]{:S(2)}) copy-start(bf16[1,8,128,128]{3,2,1,0:T(8,128)(2,1)} %param.6) | copy-start | bytes 786436
  1.0 0.7 copy-start.2
  1.6 0.7 copy-start.3
  2.3 0.7 copy-start.4
  4.0 38.9 %copy-start = (bf16[1,8,6,64,128]{4,3,2,1,0:T(8,128)(2,1)S(1)}, bf16[1,8,6,64,128]{4,3,2,1,0:T(8,128)(2,1)}, u32[]{:S(2)}) copy-start(bf16[1,8,6,64,128]{4,3,2,1,0:T(8,128)(2,1)} %param.5) | copy-start | bytes 2359300
  21.7 6.2 %collective-permute-start = (f32[72,128]{1,0:T(8,128)S(1)}, f32[72,128]{1,0:T(8,128)S(1)}, u32[]{:S(2)}, u32[]{:S(2)}) collective-permute-start(f32[72,128]{1,0:T(8,128)S(1)} %slice_reduce_fusion), channel_id=1, source_target_pairs={{0,1},{1,2},{2,3},{3,4},{4,5},{5,6},{6,7},{7,8},{8,9},{9,10},{10,1... | collective-permute-start | bytes 110600 | tf_op jit(solution)/shard_map/ppermute | solution.py:248

commit v2 on v1

v2 whole, which is shorter than its diff:
```python
import jax
import jax.numpy as jnp
from jax import lax
from jax.experimental import pallas as pl
from jax.experimental.pallas import tpu as pltpu
from jax.sharding import PartitionSpec as P

ITERS = 12
REACH = 4
RELAXATION = 0.9
EPSILON = 1e-06
MEMBERS = 128
HALF = MEMBERS // 2
PACKED = 72

bf16 = jnp.bfloat16
f32 = jnp.float32


def iota2(shape, dim):
    return lax.broadcasted_iota(jnp.int32, shape, dim)


def halves(value):
    high = value.astype(bf16)
    return high, (value - high.astype(f32)).astype(bf16)


def dot(left, right):
    return jnp.dot(left, right, preferred_element_type=f32)


def pack(gram, vector):
    row, lane = iota2((HALF, MEMBERS), 0), iota2((HALF, MEMBERS), 1)
    lower = pltpu.roll(gram[HALF:], HALF, 1)
    matrix = jnp.where(lane >= row, gram[:HALF], lower)
    diagonal = jnp.sum(jnp.where(lane == row, lower, 0.0), axis=0, keepdims=True)
    tail = iota2((8, MEMBERS), 0)
    rest = jnp.where(tail == 0, diagonal, jnp.where(tail == 1, vector, 0.0))
    return jnp.concatenate([matrix, rest], axis=0)


def unpack(packed):
    row, lane = iota2((HALF, MEMBERS), 0), iota2((HALF, MEMBERS), 1)
    matrix = packed[:HALF]
    diagonal = packed[HALF : HALF + 1]
    vector = packed[HALF + 1 : HALF + 2]
    flipped = jnp.transpose(jnp.concatenate([matrix, jnp.zeros_like(matrix)], axis=0))
    upper = jnp.where(lane >= row, matrix, flipped[:HALF])
    corner = jnp.where(lane == row, diagonal, jnp.where(lane < row, matrix, flipped[:HALF]))
    lower = jnp.where(lane < HALF, flipped[HALF:], pltpu.roll(corner, HALF, 1))
    return jnp.concatenate([upper, lower], axis=0), vector


def statistics_kernel(weight_ref, weighted_ref, ensemble_hbm, out_ref, ensemble_ref, system_ref, sem):
    patches = ensemble_ref.shape[0]
    copies = [
        pltpu.make_async_copy(ensemble_hbm.at[p], ensemble_ref.at[p], sem.at[p])
        for p in range(patches)
    ]
    for copy in copies:
        copy.start()
    for p in range(patches):
        copies[p].wait()
        ensemble = ensemble_ref[p]
        flipped = jnp.transpose(ensemble.astype(f32)) * weight_ref[p : p + 1, :]
        weighted_value = jnp.broadcast_to(weighted_ref[p : p + 1, :], (16, MEMBERS))
        high, low = halves(jnp.concatenate([flipped, weighted_value], axis=0))
        sums = dot(
            jnp.concatenate([high, low], axis=1), jnp.concatenate([ensemble, ensemble], axis=0)
        )
        system_ref[p] = pack(sums[:MEMBERS], sums[MEMBERS : MEMBERS + 1])
    for target in range(-REACH, patches + REACH):
        total = None
        for p in range(patches):
            distance = abs(target - p)
            if distance <= REACH:
                term = (1.0 - distance / (REACH + 1.0)) * system_ref[p]
                total = term if total is None else total + term
        if 0 <= target < patches:
            out_ref[target, 0] = total
        else:
            out_ref[target % patches, 1] = total


VMEM = pl.BlockSpec(memory_space=pltpu.VMEM)
HBM = pl.BlockSpec(memory_space=pltpu.HBM)
PARAMS = pltpu.CompilerParams(vmem_limit_bytes=16 * 1024 * 1024)


def statistics(obs_ensemble, obs_value, obs_weight, obs_count):
    patches, observations, members = obs_ensemble.shape
    weight = jnp.where(
        iota2(obs_weight.shape, 1) < obs_count[:, None], obs_weight.astype(f32), 0.0
    )
    return pl.pallas_call(
        statistics_kernel,
        out_shape=jax.ShapeDtypeStruct((patches, 2, PACKED, members), f32),
        in_specs=[VMEM, VMEM, HBM],
        out_specs=VMEM,
        scratch_shapes=[
            pltpu.VMEM(obs_ensemble.shape, bf16),
            pltpu.VMEM((patches, PACKED, members), f32),
            pltpu.SemaphoreType.DMA((patches,)),
        ],
        compiler_params=PARAMS,
    )(weight, weight * obs_value.astype(f32), obs_ensemble)


def solver_kernel(received_ref, beside_ref, out_ref):
    total = beside_ref[...]
    for s in range(received_ref.shape[0]):
        total = total + received_ref[s, 0]
    gram, vector = unpack(total)
    scale = 1.0 / MEMBERS
    mean_row = jnp.sum(gram, axis=0, keepdims=True) * scale
    mean_column = jnp.sum(gram, axis=1, keepdims=True) * scale
    mean_all = jnp.sum(mean_row, axis=1, keepdims=True) * scale
    vector = vector - mean_row
    vector = vector - jnp.sum(vector, axis=1, keepdims=True) * scale
    shape = (MEMBERS, MEMBERS)
    identity = jnp.where(iota2(shape, 0) == iota2(shape, 1), 1.0, 0.0)
    matrix = gram - mean_row - mean_column + mean_all + (MEMBERS - 1.0) * identity
    bound = jnp.sum(jnp.sum(jnp.abs(matrix), axis=0, keepdims=True), axis=1, keepdims=True)
    state = matrix / bound
    inverse_root = None
    for sweep in range(ITERS):
        middle = 1.5 * identity - 0.5 * state
        high, low = halves(middle)
        right = jnp.concatenate(
            [jnp.concatenate([high, low], axis=1), jnp.concatenate([low, high], axis=1)], axis=0
        )

        def times_middle(left):
            product = dot(jnp.concatenate(halves(left), axis=1), right)
            return product[:, :MEMBERS] + product[:, MEMBERS:]

        if sweep < ITERS - 1:
            state = times_middle(times_middle(state))
        inverse_root = middle if sweep == 0 else times_middle(inverse_root)
    inner = jnp.sum(inverse_root * vector, axis=1, keepdims=True)
    mean_weight = jnp.sum(inverse_root * inner, axis=0, keepdims=True) / bound
    mean_weight = jnp.sum(jnp.where(identity > 0.0, mean_weight, 0.0), axis=1, keepdims=True)
    mixing = inverse_root * jnp.sqrt((MEMBERS - 1.0) / bound) + mean_weight
    out_ref[...] = jnp.broadcast_to(mixing.astype(bf16)[None], out_ref.shape)


def solver(received, beside):
    return pl.pallas_call(
        solver_kernel,
        out_shape=jax.ShapeDtypeStruct((received.shape[0], MEMBERS, MEMBERS), bf16),
        in_specs=[VMEM, VMEM],
        out_specs=VMEM,
        compiler_params=PARAMS,
    )(received, beside)


def level_sums(squares, levels):
    return jnp.sum(squares.reshape(levels, -1, 8, MEMBERS), axis=1)


def prior_kernel(states_ref, spread_ref, center_ref, square_ref):
    patches, levels, columns, _ = states_ref.shape
    average = jnp.full((MEMBERS, MEMBERS), 1.0 / MEMBERS, bf16)
    total = None
    for p in range(patches):
        states = states_ref[p].reshape(levels * columns, MEMBERS)
        center = dot(states, average)
        spread = (states.astype(f32) - center).astype(bf16)
        spread_ref[p] = spread
        center_ref[p] = center
        square = level_sums(jnp.square(spread.astype(f32)), levels)
        total = square if total is None else total + square
    square_ref[...] = total


def prior(states):
    patches, levels, columns, members = states.shape
    rows = levels * columns
    return pl.pallas_call(
        prior_kernel,
        out_shape=(
            jax.ShapeDtypeStruct((patches, rows, members), bf16),
            jax.ShapeDtypeStruct((patches, rows, members), f32),
            jax.ShapeDtypeStruct((levels, 8, members), f32),
        ),
        in_specs=[VMEM],
        out_specs=(VMEM, VMEM, VMEM),
        compiler_params=PARAMS,
        cost_estimate=pl.CostEstimate(
            flops=2 * patches * rows * members * members, bytes_accessed=1 << 22, transcendentals=0
        ),
    )(states)


def apply_kernel(mixing_ref, prior_spread_ref, prior_center_ref, prior_square_ref, spread_ref, center_ref, sums_ref):
    patches = mixing_ref.shape[0]
    levels = prior_square_ref.shape[0]
    average = jnp.full((MEMBERS, MEMBERS), 1.0 / MEMBERS, bf16)
    total = None
    for p in range(patches):
        mixing = mixing_ref[p]
        mixing_center = dot(mixing, average)
        spread_high, spread_low = halves(mixing.astype(f32) - mixing_center)
        center_high, center_low = halves(mixing_center)
        right = jnp.concatenate(
            [
                jnp.concatenate([spread_high, center_high], axis=1),
                jnp.concatenate([spread_low, center_low], axis=1),
            ],
            axis=0,
        )
        prior_spread = prior_spread_ref[p]
        product = dot(jnp.concatenate([prior_spread, prior_spread], axis=1), right)
        post_spread = product[:, :MEMBERS]
        spread_ref[p] = post_spread
        center_ref[p] = prior_center_ref[p] + product[:, MEMBERS:]
        square = level_sums(jnp.square(post_spread), levels)
        total = square if total is None else total + square
    sums = jnp.concatenate(
        [jnp.sum(prior_square_ref[...], axis=1), jnp.sum(total, axis=1),
         jnp.zeros((MEMBERS - 2 * levels, MEMBERS), f32)], axis=0
    )
    sums = jnp.sum(jnp.transpose(sums), axis=0, keepdims=True)
    sums_ref[...] = jnp.broadcast_to(sums, sums_ref.shape)


def apply_weights(mixing, prior_spread, prior_center, prior_square, receivers):
    patches, rows, members = prior_spread.shape
    return pl.pallas_call(
        apply_kernel,
        out_shape=(
            jax.ShapeDtypeStruct((patches, rows, members), f32),
            jax.ShapeDtypeStruct((patches, rows, members), f32),
            jax.ShapeDtypeStruct((receivers, members), f32),
        ),
        in_specs=[VMEM] * 4,
        out_specs=(VMEM, VMEM, VMEM),
        compiler_params=PARAMS,
    )(mixing, prior_spread, prior_center, prior_square)


def finish_kernel(divisor, sums_ref, spread_ref, center_ref, out_hbm, out_ref, out_sem):
    patches, levels, columns, _ = out_ref.shape
    sums = jnp.sum(sums_ref[...], axis=0, keepdims=True)
    deviation = jnp.sqrt(sums / divisor + EPSILON)
    lane = iota2(deviation.shape, 1)
    factors = []
    for level in range(levels):
        prior_sd = jnp.sum(jnp.where(lane == level, deviation, 0.0), axis=1, keepdims=True)
        post_sd = jnp.sum(jnp.where(lane == levels + level, deviation, 0.0), axis=1, keepdims=True)
        factors.append(1.0 + RELAXATION * (prior_sd - post_sd) / post_sd)
    copies = []
    for p in range(patches):
        for level in range(levels):
            rows = pl.ds(level * columns, columns)
            result = center_ref[p, rows] + factors[level] * spread_ref[p, rows]
            out_ref[p, level] = result.astype(bf16)
        copies.append(pltpu.make_async_copy(out_ref.at[p], out_hbm.at[p], out_sem.at[p]))
        copies[-1].start()
    for copy in copies:
        copy.wait()


def finish(sums, spread, center, shape, divisor):
    def kernel(*refs):
        finish_kernel(divisor, *refs)

    return pl.pallas_call(
        kernel,
        out_shape=jax.ShapeDtypeStruct(shape, bf16),
        in_specs=[VMEM] * 3,
        out_specs=HBM,
        scratch_shapes=[pltpu.VMEM(shape, bf16), pltpu.SemaphoreType.DMA((shape[0],))],
        compiler_params=PARAMS,
    )(sums, spread, center)


def shards(background, obs_ensemble, obs_value, obs_weight, obs_count):
    lags, tiles = lax.axis_size("lag"), lax.axis_size("col")
    patches, columns = background.shape[1], background.shape[3]
    sent = statistics(obs_ensemble[0], obs_value[0], obs_weight[0], obs_count[0])
    received = lax.all_to_all(sent, "lag", 0, 0)
    beside = jnp.sum(received[:, 1], axis=0)
    moves = [
        (i * tiles + c, i * tiles + (c + (1 if i < REACH else -1)) % tiles)
        for i in range(lags)
        for c in range(tiles)
    ]
    states, beside = lax.optimization_barrier((background[0], beside))
    beside = lax.ppermute(beside, ("lag", "col"), moves)
    prior_spread, prior_center, prior_square = prior(states)
    beside, prior_square = lax.optimization_barrier((beside, prior_square))
    mixing = lax.all_to_all(solver(received, beside), "lag", 0, 0)
    spread, center, sums = apply_weights(mixing, prior_spread, prior_center, prior_square, tiles)
    sums = lax.all_to_all(sums, "col", 0, 0, tiled=True)
    divisor = (MEMBERS - 1.0) * patches * tiles * columns
    return finish(sums, spread, center, background.shape[1:], divisor)[None]


def solution(mesh):
    placed = (
        P("lag", "col", None, None, None),
        P("lag", "col", None, None),
        P("lag", "col", None),
        P("lag", "col", None),
        P("lag", "col"),
    )
    return jax.shard_map(
        shards,
        mesh=mesh,
        in_specs=placed,
        out_specs=P("lag", "col", None, None, None),
        check_vma=False,
    )
```

time: 82.5 us -> 79.1 us (0.959)
  local copies, waits for them, and re-layouts: 2.97 us -> 0.95 us
  Pallas kernels: 11.2 us -> 9.63 us
  other arithmetic: 0.02 us -> 0.86 us
    pallas_call x2 -> x3, Pallas kernels: 6.17 us -> 2.82 us  [the longest x1 1.3 us: apply_weights(): pl.pallas_call(apply_kernel, out_shape=(jax.ShapeDtypeStruct((patches, ro...]
    unnamed x10 -> x4, local copies, waits for them, and re-layouts: 2.97 us -> 0.95 us
    pallas_call x1, Pallas kernels: 1.02 us -> 2.82 us  [statistics(): pl.pallas_call(statistics_kernel, out_shape=jax.ShapeDtypeStruct((patches...]
    mul x0 -> x1, other arithmetic: none -> 0.84 us  [statistics(): weight * obs_value.astype(f32)]
  transfers between devices with their start and end apart: 1 -> 1, of which waited for: 1 -> 1; matrix products, arithmetic and copies ran while one was open for 0% -> 0% of each run, Pallas kernels for 0% -> 1%
where the time goes in v2:
time: 79.1 us; the launch traced here: 78.9 us
  blocking collectives  61.6 us (78%)
  Pallas kernels  9.63 us (12%)
  starting transfers between devices  5.19 us (7%)
  local copies, waits for them, and re-layouts  0.95 us (1%)
  other arithmetic  0.86 us (1%)
    all_to_all x1, blocking collectives, shards(): sums = lax.all_to_all(sums, 'col', 0, 0, tiled=True)  33.1 us
    all_to_all x1, blocking collectives, shards(): received = lax.all_to_all(sent, 'lag', 0, 0)  17.6 us
    all_to_all x1, blocking collectives, shards(): mixing = lax.all_to_all(solver(received, beside), 'lag', 0, 0)  10.9 us
    ppermute x1, starting transfers between devices, shards(): beside = lax.ppermute(beside, ('lag', 'col'), moves)  5.19 us
    pallas_call x1, Pallas kernels, solver(): pl.pallas_call(solver_kernel, out_shape=jax.ShapeDtypeStruct((received.sh...  3.99 us
    pallas_call x1, Pallas kernels, statistics(): pl.pallas_call(statistics_kernel, out_shape=jax.ShapeDtypeStruct((patches...  2.82 us
  transfers between devices with their start and end apart: 1, of which 1 were waited for; matrix products, arithmetic and copies ran while one was open for 0% of the time, Pallas kernels for 1%

profile of v2, /device:TPU:1, one launch (start us, length us, event | category | flops | bytes accessed | tf_op | source)
XLA Modules:
  0.0 78.9 jit_solution(13817827626050778437)
XLA Ops:
  0.0 0.0 copy-start
  0.0 0.8 %convert_multiply_fusion = (f32[8,128]{1,0:T(8,128)S(1)}, f32[8,128]{1,0:T(8,128)S(1)}) fusion(bf16[1,8,128]{2,1,0:T(8,128)(2,1)} %param.7, bf16[1,8,128]{2,1,0:T(8,128)(2,1)} %param.8, s32[8]{0:T(128)} %bitcast.20), kind=kLoop, calls=%fused_computation.1 | loop fusion | flops 5120 | bytes 12320 | tf_op jit(solution)/shard_map/mul | solution.py:107
  0.8 0.0 copy-start.1
  0.8 0.9 %copy-done.1 = bf16[1,8,128,128]{3,2,1,0:T(8,128)(2,1)S(1)} copy-done((bf16[1,8,128,128]{3,2,1,0:T(8,128)(2,1)S(1)}, bf16[1,8,128,128]{3,2,1,0:T(8,128)(2,1)}, u32[]{:S(2)}) %copy-start.1) | copy-done | bytes 262168
  1.8 2.8 %shard_map.55 = f32[8,2,72,128]{3,2,1,0:T(8,128)S(1)} custom-call(f32[8,128]{1,0:T(8,128)S(1)} %get-tuple-element.26.weight_ref, f32[8,128]{1,0:T(8,128)S(1)} %get-tuple-element.25.weighted_ref, bf16[8,128,128]{2,1,0:T(8,128)(2,1)S(1)} %bitcast.17), custom_call_target="tpu_custom_call" | custom-call | tf_op jit(solution)/shard_map/pallas_call | solution.py:96
  4.6 17.6 %all_to_all.21.received_ref = f32[8,2,72,128]{3,2,1,0:T(8,128)S(1)} all-to-all(f32[8,2,72,128]{3,2,1,0:T(8,128)S(1)} %shard_map.55), channel_id=1, replica_groups=mesh['lag'=8,'col'=64] {'lag'}, dimensions={0} | all-to-all | bytes 1179648 | tf_op jit(solution)/shard_map/all_to_all | solution.py:283
  22.2 5.2 %collective-permute-start = (f32[72,128]{1,0:T(8,128)S(1)}, f32[72,128]{1,0:T(8,128)S(1)}, u32[]{:S(2)}, u32[]{:S(2)}) collective-permute-start(f32[72,128]{1,0:T(8,128)S(1)} %slice_reduce_fusion), channel_id=1, source_target_pairs={{0,1},{1,2},{2,3},{3,4},{4,5},{5,6},{6,7},{7,8},{8,9},{9,10},{10,1... | collective-permute-start | bytes 110600 | tf_op jit(solution)/shard_map/ppermute | solution.py:291
  27.4 0.0 copy-done
  27.4 0.4 shard_map.56
  27.9 0.6 collective-permute-done.beside_ref
  28.4 4.0 %shard_map.57 = bf16[8,128,128]{2,1,0:T(8,128)(2,1)S(1)} custom-call(f32[8,2,72,128]{3,2,1,0:T(8,128)S(1)} %all_to_all.21.received_ref, f32[72,128]{1,0:T(8,128)S(1)} %collective-permute-done.beside_ref), custom_call_target="tpu_custom_call" | custom-call | tf_op jit(solution)/shard_map/pallas_call | solution.py:149
  32.4 10.9 %all_to_all.22.mixing_ref = bf16[8,128,128]{2,1,0:T(8,128)(2,1)S(1)} all-to-all(bf16[8,128,128]{2,1,0:T(8,128)(2,1)S(1)} %shard_map.57), channel_id=1, replica_groups=mesh['lag'=8,'col'=64] {'lag'}, dimensions={0} | all-to-all | bytes 524288 | tf_op jit(solution)/shard_map/all_to_all | solution.py:294
  43.4 1.3 %shard_map.58 = (f32[8,384,128]{2,1,0:T(8,128)S(1)}, f32[8,384,128]{2,1,0:T(8,128)S(1)}, f32[64,128]{1,0:T(8,128)S(1)}) custom-call(bf16[8,128,128]{2,1,0:T(8,128)(2,1)S(1)} %all_to_all.22.mixing_ref, bf16[8,384,128]{2,1,0:T(8,128)(2,1)S(1)} %get-tuple-element.19.prior_spread_ref, f32[8,384,128]{2,1,0:T(8,128)S(1)} %get-tuple-element.20.prior_center_ref, ...), custom_call_target="tpu_custom_call" | custom-call | tf_op jit(solution)/shard_map/pallas_call | solution.py:230
  44.7 33.1 %all_to_all.23 = f32[64,1,128]{2,1,0:T(1,128)S(1)} all-to-all(f32[64,1,128]{2,1,0:T(1,128)S(1)} %bitcast.19), channel_id=1, replica_groups=mesh['lag'=8,'col'=64] {'col'}, dimensions={0} | all-to-all | bytes 65536 | tf_op jit(solution)/shard_map/all_to_all | solution.py:296
  77.8 1.1 %shard_map.59 = bf16[8,6,64,128]{3,2,1,0:T(8,128)(2,1)} custom-call(f32[64,128]{1,0:T(8,128)S(1)} %bitcast.18, f32[8,384,128]{2,1,0:T(8,128)S(1)} %get-tuple-element.23.refs_1_, f32[8,384,128]{2,1,0:T(8,128)S(1)} %get-tuple-element.24.refs_2_), custom_call_target="tpu_custom_call" | custom-call | tf_op jit(solution)/shard_map/pallas_call | solution.py:269
  (1 shorter events, 0.0 us)
Async XLA Ops:
  0.0 27.4 %copy-start = (bf16[1,8,6,64,128]{4,3,2,1,0:T(8,128)(2,1)S(1)}, bf16[1,8,6,64,128]{4,3,2,1,0:T(8,128)(2,1)}, u32[]{:S(2)}) copy-start(bf16[1,8,6,64,128]{4,3,2,1,0:T(8,128)(2,1)} %param.5) | copy-start | bytes 2359300
  0.8 1.0 %copy-start.1 = (bf16[1,8,128,128]{3,2,1,0:T(8,128)(2,1)S(1)}, bf16[1,8,128,128]{3,2,1,0:T(8,128)(2,1)}, u32[]{:S(2)}) copy-start(bf16[1,8,128,128]{3,2,1,0:T(8,128)(2,1)} %param.6) | copy-start | bytes 786436
  22.2 6.2 %collective-permute-start = (f32[72,128]{1,0:T(8,128)S(1)}, f32[72,128]{1,0:T(8,128)S(1)}, u32[]{:S(2)}, u32[]{:S(2)}) collective-permute-start(f32[72,128]{1,0:T(8,128)S(1)} %slice_reduce_fusion), channel_id=1, source_target_pairs={{0,1},{1,2},{2,3},{3,4},{4,5},{5,6},{6,7},{7,8},{8,9},{9,10},{10,1... | collective-permute-start | bytes 110600 | tf_op jit(solution)/shard_map/ppermute | solution.py:291

commit v3 on v2

--- a/solution.py
+++ b/solution.py
@@ -52,16 +52,9 @@
     return jnp.concatenate([upper, lower], axis=0), vector
 
 
-def statistics_kernel(weight_ref, weighted_ref, ensemble_hbm, out_ref, ensemble_ref, system_ref, sem):
+def statistics_kernel(weight_ref, weighted_ref, ensemble_ref, out_ref, system_ref):
     patches = ensemble_ref.shape[0]
-    copies = [
-        pltpu.make_async_copy(ensemble_hbm.at[p], ensemble_ref.at[p], sem.at[p])
-        for p in range(patches)
-    ]
-    for copy in copies:
-        copy.start()
     for p in range(patches):
-        copies[p].wait()
         ensemble = ensemble_ref[p]
         flipped = jnp.transpose(ensemble.astype(f32)) * weight_ref[p : p + 1, :]
         weighted_value = jnp.broadcast_to(weighted_ref[p : p + 1, :], (16, MEMBERS))
@@ -96,12 +89,10 @@
     return pl.pallas_call(
         statistics_kernel,
         out_shape=jax.ShapeDtypeStruct((patches, 2, PACKED, members), f32),
-        in_specs=[VMEM, VMEM, HBM],
+        in_specs=[VMEM] * 3,
         out_specs=VMEM,
         scratch_shapes=[
-            pltpu.VMEM(obs_ensemble.shape, bf16),
             pltpu.VMEM((patches, PACKED, members), f32),
-            pltpu.SemaphoreType.DMA((patches,)),
         ],
         compiler_params=PARAMS,
     )(weight, weight * obs_value.astype(f32), obs_ensemble)

time: 79.1 us -> 76.8 us (0.971)
  Pallas kernels: 9.63 us -> 7.28 us
    pallas_call x1, Pallas kernels: 2.82 us -> 0.47 us  [statistics(): pl.pallas_call(statistics_kernel, out_shape=jax.ShapeDtypeStruct((patches...]
where the time goes in v3:
time: 76.8 us; the launch traced here: 76.5 us
  blocking collectives  61.6 us (80%)
  Pallas kernels  7.28 us (9%)
  starting transfers between devices  5.19 us (7%)
  local copies, waits for them, and re-layouts  0.95 us (1%)
  other arithmetic  0.86 us (1%)
    all_to_all x1, blocking collectives, shards(): sums = lax.all_to_all(sums, 'col', 0, 0, tiled=True)  33.1 us
    all_to_all x1, blocking collectives, shards(): received = lax.all_to_all(sent, 'lag', 0, 0)  17.5 us
    all_to_all x1, blocking collectives, shards(): mixing = lax.all_to_all(solver(received, beside), 'lag', 0, 0)  10.9 us
    ppermute x1, starting transfers between devices, shards(): beside = lax.ppermute(beside, ('lag', 'col'), moves)  5.19 us
    pallas_call x1, Pallas kernels, solver(): pl.pallas_call(solver_kernel, out_shape=jax.ShapeDtypeStruct((received.sh...  3.99 us
  transfers between devices with their start and end apart: 1, of which 1 were waited for; matrix products, arithmetic and copies ran while one was open for 0% of the time, Pallas kernels for 1%

profile of v3, /device:TPU:1, one launch (start us, length us, event | category | flops | bytes accessed | tf_op | source)
XLA Modules:
  0.0 76.5 jit_solution(13172502689572907212)
XLA Ops:
  0.0 0.0 copy-start
  0.0 0.8 %convert_multiply_fusion = (f32[8,128]{1,0:T(8,128)S(1)}, f32[8,128]{1,0:T(8,128)S(1)}) fusion(bf16[1,8,128]{2,1,0:T(8,128)(2,1)} %param.7, bf16[1,8,128]{2,1,0:T(8,128)(2,1)} %param.8, s32[8]{0:T(128)} %bitcast.20), kind=kLoop, calls=%fused_computation.1 | loop fusion | flops 5120 | bytes 12320 | tf_op jit(solution)/shard_map/mul | solution.py:98
  0.8 0.0 copy-start.1
  0.8 0.9 %copy-done.1 = bf16[1,8,128,128]{3,2,1,0:T(8,128)(2,1)S(1)} copy-done((bf16[1,8,128,128]{3,2,1,0:T(8,128)(2,1)S(1)}, bf16[1,8,128,128]{3,2,1,0:T(8,128)(2,1)}, u32[]{:S(2)}) %copy-start.1) | copy-done | bytes 262168
  1.8 0.5 shard_map.55
  2.3 17.5 %all_to_all.21.received_ref = f32[8,2,72,128]{3,2,1,0:T(8,128)S(1)} all-to-all(f32[8,2,72,128]{3,2,1,0:T(8,128)S(1)} %shard_map.55), channel_id=1, replica_groups=mesh['lag'=8,'col'=64] {'lag'}, dimensions={0} | all-to-all | bytes 1179648 | tf_op jit(solution)/shard_map/all_to_all | solution.py:274
  19.8 5.2 %collective-permute-start = (f32[72,128]{1,0:T(8,128)S(1)}, f32[72,128]{1,0:T(8,128)S(1)}, u32[]{:S(2)}, u32[]{:S(2)}) collective-permute-start(f32[72,128]{1,0:T(8,128)S(1)} %slice_reduce_fusion), channel_id=1, source_target_pairs={{0,1},{1,2},{2,3},{3,4},{4,5},{5,6},{6,7},{7,8},{8,9},{9,10},{10,1... | collective-permute-start | bytes 110600 | tf_op jit(solution)/shard_map/ppermute | solution.py:282
  25.1 0.0 copy-done
  25.1 0.4 shard_map.56
  25.5 0.6 collective-permute-done.beside_ref
  26.1 4.0 %shard_map.57 = bf16[8,128,128]{2,1,0:T(8,128)(2,1)S(1)} custom-call(f32[8,2,72,128]{3,2,1,0:T(8,128)S(1)} %all_to_all.21.received_ref, f32[72,128]{1,0:T(8,128)S(1)} %collective-permute-done.beside_ref), custom_call_target="tpu_custom_call" | custom-call | tf_op jit(solution)/shard_map/pallas_call | solution.py:140
  30.1 10.9 %all_to_all.22.mixing_ref = bf16[8,128,128]{2,1,0:T(8,128)(2,1)S(1)} all-to-all(bf16[8,128,128]{2,1,0:T(8,128)(2,1)S(1)} %shard_map.57), channel_id=1, replica_groups=mesh['lag'=8,'col'=64] {'lag'}, dimensions={0} | all-to-all | bytes 524288 | tf_op jit(solution)/shard_map/all_to_all | solution.py:285
  41.0 1.3 %shard_map.58 = (f32[8,384,128]{2,1,0:T(8,128)S(1)}, f32[8,384,128]{2,1,0:T(8,128)S(1)}, f32[64,128]{1,0:T(8,128)S(1)}) custom-call(bf16[8,128,128]{2,1,0:T(8,128)(2,1)S(1)} %all_to_all.22.mixing_ref, bf16[8,384,128]{2,1,0:T(8,128)(2,1)S(1)} %get-tuple-element.19.prior_spread_ref, f32[8,384,128]{2,1,0:T(8,128)S(1)} %get-tuple-element.20.prior_center_ref, ...), custom_call_target="tpu_custom_call" | custom-call | tf_op jit(solution)/shard_map/pallas_call | solution.py:221
  42.3 33.1 %all_to_all.23 = f32[64,1,128]{2,1,0:T(1,128)S(1)} all-to-all(f32[64,1,128]{2,1,0:T(1,128)S(1)} %bitcast.19), channel_id=1, replica_groups=mesh['lag'=8,'col'=64] {'col'}, dimensions={0} | all-to-all | bytes 65536 | tf_op jit(solution)/shard_map/all_to_all | solution.py:287
  75.4 1.1 %shard_map.59 = bf16[8,6,64,128]{3,2,1,0:T(8,128)(2,1)} custom-call(f32[64,128]{1,0:T(8,128)S(1)} %bitcast.18, f32[8,384,128]{2,1,0:T(8,128)S(1)} %get-tuple-element.23.refs_1_, f32[8,384,128]{2,1,0:T(8,128)S(1)} %get-tuple-element.24.refs_2_), custom_call_target="tpu_custom_call" | custom-call | tf_op jit(solution)/shard_map/pallas_call | solution.py:260
  (1 shorter events, 0.0 us)
Async XLA Ops:
  0.0 25.1 %copy-start = (bf16[1,8,6,64,128]{4,3,2,1,0:T(8,128)(2,1)S(1)}, bf16[1,8,6,64,128]{4,3,2,1,0:T(8,128)(2,1)}, u32[]{:S(2)}) copy-start(bf16[1,8,6,64,128]{4,3,2,1,0:T(8,128)(2,1)} %param.5) | copy-start | bytes 2359300
  0.8 1.0 %copy-start.1 = (bf16[1,8,128,128]{3,2,1,0:T(8,128)(2,1)S(1)}, bf16[1,8,128,128]{3,2,1,0:T(8,128)(2,1)}, u32[]{:S(2)}) copy-start(bf16[1,8,128,128]{3,2,1,0:T(8,128)(2,1)} %param.6) | copy-start | bytes 786436
  19.8 6.2 %collective-permute-start = (f32[72,128]{1,0:T(8,128)S(1)}, f32[72,128]{1,0:T(8,128)S(1)}, u32[]{:S(2)}, u32[]{:S(2)}) collective-permute-start(f32[72,128]{1,0:T(8,128)S(1)} %slice_reduce_fusion), channel_id=1, source_target_pairs={{0,1},{1,2},{2,3},{3,4},{4,5},{5,6},{6,7},{7,8},{8,9},{9,10},{10,1... | collective-permute-start | bytes 110600 | tf_op jit(solution)/shard_map/ppermute | solution.py:282

commit v4 on v2

--- a/solution.py
+++ b/solution.py
@@ -52,20 +52,34 @@
     return jnp.concatenate([upper, lower], axis=0), vector
 
 
-def statistics_kernel(weight_ref, weighted_ref, ensemble_hbm, out_ref, ensemble_ref, system_ref, sem):
+def statistics_kernel(
+    count_hbm, weight_hbm, value_hbm, ensemble_hbm, out_ref,
+    count_ref, weight_ref, value_ref, ensemble_ref, system_ref, sem,
+):
     patches = ensemble_ref.shape[0]
+    arrays = [(count_hbm, count_ref), (weight_hbm, weight_ref), (value_hbm, value_ref)]
+    parts = [(ensemble_hbm, ensemble_ref)]
     copies = [
-        pltpu.make_async_copy(ensemble_hbm.at[p], ensemble_ref.at[p], sem.at[p])
-        for p in range(patches)
+        pltpu.make_async_copy(source, target, sem.at[i])
+        for i, (source, target) in enumerate(parts + arrays)
     ]
     for copy in copies:
         copy.start()
+    for copy in copies[1:]:
+        copy.wait()
+    lane = iota2((1, MEMBERS), 1)
     for p in range(patches):
-        copies[p].wait()
+        if p == 0:
+            copies[0].wait()
+        weight = weight_ref[p : p + 1, :].astype(f32)
+        weight = jnp.where(lane < count_ref[:, p : p + 1], weight, 0.0)
+        weighted_value = weight * value_ref[p : p + 1, :].astype(f32)
         ensemble = ensemble_ref[p]
-        flipped = jnp.transpose(ensemble.astype(f32)) * weight_ref[p : p + 1, :]
-        weighted_value = jnp.broadcast_to(weighted_ref[p : p + 1, :], (16, MEMBERS))
-        high, low = halves(jnp.concatenate([flipped, weighted_value], axis=0))
+        flipped = jnp.transpose(ensemble.astype(f32)) * weight
+        rows = jnp.concatenate(
+            [flipped, jnp.broadcast_to(weighted_value, (16, MEMBERS))], axis=0
+        )
+        high, low = halves(rows)
         sums = dot(
             jnp.concatenate([high, low], axis=1), jnp.concatenate([ensemble, ensemble], axis=0)
         )
@@ -88,23 +102,25 @@
 PARAMS = pltpu.CompilerParams(vmem_limit_bytes=16 * 1024 * 1024)
 
 
-def statistics(obs_ensemble, obs_value, obs_weight, obs_count):
+def statistics(obs_count, obs_weight, obs_value, obs_ensemble):
     patches, observations, members = obs_ensemble.shape
-    weight = jnp.where(
-        iota2(obs_weight.shape, 1) < obs_count[:, None], obs_weight.astype(f32), 0.0
-    )
+    operands = (obs_count, obs_weight, obs_value, obs_ensemble)
+    operands = [pltpu.with_memory_space_constraint(x, pltpu.HBM) for x in operands]
     return pl.pallas_call(
         statistics_kernel,
         out_shape=jax.ShapeDtypeStruct((patches, 2, PACKED, members), f32),
-        in_specs=[VMEM, VMEM, HBM],
+        in_specs=[HBM] * 4,
         out_specs=VMEM,
         scratch_shapes=[
+            pltpu.VMEM(obs_count.shape, jnp.int32),
+            pltpu.VMEM(obs_weight.shape, bf16),
+            pltpu.VMEM(obs_value.shape, bf16),
             pltpu.VMEM(obs_ensemble.shape, bf16),
             pltpu.VMEM((patches, PACKED, members), f32),
-            pltpu.SemaphoreType.DMA((patches,)),
+            pltpu.SemaphoreType.DMA((4,)),
         ],
         compiler_params=PARAMS,
-    )(weight, weight * obs_value.astype(f32), obs_ensemble)
+    )(*operands)
 
 
 def solver_kernel(received_ref, beside_ref, out_ref):
@@ -279,7 +295,7 @@
 def shards(background, obs_ensemble, obs_value, obs_weight, obs_count):
     lags, tiles = lax.axis_size("lag"), lax.axis_size("col")
     patches, columns = background.shape[1], background.shape[3]
-    sent = statistics(obs_ensemble[0], obs_value[0], obs_weight[0], obs_count[0])
+    sent = statistics(obs_count, obs_weight[0], obs_value[0], obs_ensemble[0])
     received = lax.all_to_all(sent, "lag", 0, 0)
     beside = jnp.sum(received[:, 1], axis=0)
     moves = [

time: 79.1 us -> 76.1 us (0.962)
  Pallas kernels: 9.63 us -> 8.38 us
  local copies, waits for them, and re-layouts: 0.95 us -> 0.01 us
  other arithmetic: 0.86 us -> 0.02 us
    pallas_call x1, Pallas kernels: 2.82 us -> 1.56 us  [statistics(): pl.pallas_call(statistics_kernel, out_shape=jax.ShapeDtypeStruct((patches...]
    unnamed x4 -> x2, local copies, waits for them, and re-layouts: 0.95 us -> 0.01 us
    mul x1 -> x0, other arithmetic: 0.84 us -> none  [statistics(): weight * obs_value.astype(f32)]
where the time goes in v4:
time: 76.1 us; the launch traced here: 75.8 us
  blocking collectives  61.6 us (81%)
  Pallas kernels  8.38 us (11%)
  starting transfers between devices  5.2 us (7%)
    all_to_all x1, blocking collectives, shards(): sums = lax.all_to_all(sums, 'col', 0, 0, tiled=True)  33.1 us
    all_to_all x1, blocking collectives, shards(): received = lax.all_to_all(sent, 'lag', 0, 0)  17.5 us
    all_to_all x1, blocking collectives, shards(): mixing = lax.all_to_all(solver(received, beside), 'lag', 0, 0)  10.9 us
    ppermute x1, starting transfers between devices, shards(): beside = lax.ppermute(beside, ('lag', 'col'), moves)  5.2 us
    pallas_call x1, Pallas kernels, solver(): pl.pallas_call(solver_kernel, out_shape=jax.ShapeDtypeStruct((received.sh...  3.99 us
    pallas_call x1, Pallas kernels, statistics(): pl.pallas_call(statistics_kernel, out_shape=jax.ShapeDtypeStruct((patches...  1.56 us
  transfers between devices with their start and end apart: 1, of which 1 were waited for; matrix products, arithmetic and copies ran while one was open for 0% of the time, Pallas kernels for 1%

profile of v4, /device:TPU:1, one launch (start us, length us, event | category | flops | bytes accessed | tf_op | source)
XLA Modules:
  0.0 75.8 jit_solution(7181335099851120281)
XLA Ops:
  0.0 0.0 copy-start
  0.0 1.6 %shard_map.55 = f32[8,2,72,128]{3,2,1,0:T(8,128)S(1)} custom-call(s32[1,8]{1,0:T(1,128)} %count_hbm.1, bf16[8,128]{1,0:T(8,128)(2,1)} %bitcast.13, bf16[8,128]{1,0:T(8,128)(2,1)} %bitcast.14, bf16[8,128,128]{2,1,0:T(8,128)(2,1)} %bitcast.12), custom_call_target="tpu_custom_call" | custom-call | tf_op jit(solution)/shard_map/pallas_call | solution.py:109
  1.6 17.5 %all_to_all.21.received_ref = f32[8,2,72,128]{3,2,1,0:T(8,128)S(1)} all-to-all(f32[8,2,72,128]{3,2,1,0:T(8,128)S(1)} %shard_map.55), channel_id=1, replica_groups=mesh['lag'=8,'col'=64] {'lag'}, dimensions={0} | all-to-all | bytes 1179648 | tf_op jit(solution)/shard_map/all_to_all | solution.py:299
  19.1 5.2 %collective-permute-start = (f32[72,128]{1,0:T(8,128)S(1)}, f32[72,128]{1,0:T(8,128)S(1)}, u32[]{:S(2)}, u32[]{:S(2)}) collective-permute-start(f32[72,128]{1,0:T(8,128)S(1)} %slice_reduce_fusion), channel_id=1, source_target_pairs={{0,1},{1,2},{2,3},{3,4},{4,5},{5,6},{6,7},{7,8},{8,9},{9,10},{10,1... | collective-permute-start | bytes 110600 | tf_op jit(solution)/shard_map/ppermute | solution.py:307
  24.3 0.0 copy-done
  24.4 0.4 shard_map.56
  24.8 0.6 collective-permute-done.beside_ref
  25.4 4.0 %shard_map.57 = bf16[8,128,128]{2,1,0:T(8,128)(2,1)S(1)} custom-call(f32[8,2,72,128]{3,2,1,0:T(8,128)S(1)} %all_to_all.21.received_ref, f32[72,128]{1,0:T(8,128)S(1)} %collective-permute-done.beside_ref), custom_call_target="tpu_custom_call" | custom-call | tf_op jit(solution)/shard_map/pallas_call | solution.py:165
  29.4 10.9 %all_to_all.22.mixing_ref = bf16[8,128,128]{2,1,0:T(8,128)(2,1)S(1)} all-to-all(bf16[8,128,128]{2,1,0:T(8,128)(2,1)S(1)} %shard_map.57), channel_id=1, replica_groups=mesh['lag'=8,'col'=64] {'lag'}, dimensions={0} | all-to-all | bytes 524288 | tf_op jit(solution)/shard_map/all_to_all | solution.py:310
  40.3 1.3 %shard_map.58 = (f32[8,384,128]{2,1,0:T(8,128)S(1)}, f32[8,384,128]{2,1,0:T(8,128)S(1)}, f32[64,128]{1,0:T(8,128)S(1)}) custom-call(bf16[8,128,128]{2,1,0:T(8,128)(2,1)S(1)} %all_to_all.22.mixing_ref, bf16[8,384,128]{2,1,0:T(8,128)(2,1)S(1)} %get-tuple-element.19.prior_spread_ref, f32[8,384,128]{2,1,0:T(8,128)S(1)} %get-tuple-element.20.prior_center_ref, ...), custom_call_target="tpu_custom_call" | custom-call | tf_op jit(solution)/shard_map/pallas_call | solution.py:246
  41.6 33.1 %all_to_all.23 = f32[64,1,128]{2,1,0:T(1,128)S(1)} all-to-all(f32[64,1,128]{2,1,0:T(1,128)S(1)} %bitcast.11), channel_id=1, replica_groups=mesh['lag'=8,'col'=64] {'col'}, dimensions={0} | all-to-all | bytes 65536 | tf_op jit(solution)/shard_map/all_to_all | solution.py:312
  74.7 1.1 %shard_map.59 = bf16[8,6,64,128]{3,2,1,0:T(8,128)(2,1)} custom-call(f32[64,128]{1,0:T(8,128)S(1)} %bitcast.10, f32[8,384,128]{2,1,0:T(8,128)S(1)} %get-tuple-element.23.refs_1_, f32[8,384,128]{2,1,0:T(8,128)S(1)} %get-tuple-element.24.refs_2_), custom_call_target="tpu_custom_call" | custom-call | tf_op jit(solution)/shard_map/pallas_call | solution.py:285
  (1 shorter events, 0.0 us)
Async XLA Ops:
  0.0 24.3 %copy-start = (bf16[1,8,6,64,128]{4,3,2,1,0:T(8,128)(2,1)S(1)}, bf16[1,8,6,64,128]{4,3,2,1,0:T(8,128)(2,1)}, u32[]{:S(2)}) copy-start(bf16[1,8,6,64,128]{4,3,2,1,0:T(8,128)(2,1)} %param.5) | copy-start | bytes 2359300
  19.1 6.2 %collective-permute-start = (f32[72,128]{1,0:T(8,128)S(1)}, f32[72,128]{1,0:T(8,128)S(1)}, u32[]{:S(2)}, u32[]{:S(2)}) collective-permute-start(f32[72,128]{1,0:T(8,128)S(1)} %slice_reduce_fusion), channel_id=1, source_target_pairs={{0,1},{1,2},{2,3},{3,4},{4,5},{5,6},{6,7},{7,8},{8,9},{9,10},{10,1... | collective-permute-start | bytes 110600 | tf_op jit(solution)/shard_map/ppermute | solution.py:307

commit v5 on v4

--- a/solution.py
+++ b/solution.py
@@ -28,6 +28,18 @@
 
 def dot(left, right):
     return jnp.dot(left, right, preferred_element_type=f32)
+
+
+def cross(right):
+    high, low = halves(right)
+    return jnp.concatenate(
+        [jnp.concatenate([high, low], axis=1), jnp.concatenate([low, high], axis=1)], axis=0
+    )
+
+
+def product(left, crossed):
+    both = dot(jnp.concatenate(halves(left), axis=1), crossed)
+    return both[:, :MEMBERS] + both[:, MEMBERS:]
 
 
 def pack(gram, vector):
@@ -68,21 +80,23 @@
     for copy in copies[1:]:
         copy.wait()
     lane = iota2((1, MEMBERS), 1)
+    copies[0].wait()
     for p in range(patches):
-        if p == 0:
-            copies[0].wait()
         weight = weight_ref[p : p + 1, :].astype(f32)
         weight = jnp.where(lane < count_ref[:, p : p + 1], weight, 0.0)
-        weighted_value = weight * value_ref[p : p + 1, :].astype(f32)
-        ensemble = ensemble_ref[p]
-        flipped = jnp.transpose(ensemble.astype(f32)) * weight
-        rows = jnp.concatenate(
-            [flipped, jnp.broadcast_to(weighted_value, (16, MEMBERS))], axis=0
+        flipped = jnp.transpose(ensemble_ref[p].astype(f32))
+        center = jnp.sum(flipped, axis=0, keepdims=True) * (1.0 / MEMBERS)
+        spread = flipped - center
+        innovation = value_ref[p : p + 1, :].astype(f32) - center
+        innovation = jnp.broadcast_to(innovation, (16, MEMBERS))
+        rows = jnp.concatenate([spread, innovation], axis=0) * weight
+        both = lax.dot_general(
+            jnp.concatenate(halves(rows), axis=1),
+            cross(spread),
+            (((1,), (1,)), ((), ())),
+            preferred_element_type=f32,
         )
-        high, low = halves(rows)
-        sums = dot(
-            jnp.concatenate([high, low], axis=1), jnp.concatenate([ensemble, ensemble], axis=0)
-        )
+        sums = both[:, :MEMBERS] + both[:, MEMBERS:]
         system_ref[p] = pack(sums[:MEMBERS], sums[MEMBERS : MEMBERS + 1])
     for target in range(-REACH, patches + REACH):
         total = None
@@ -128,32 +142,18 @@
     for s in range(received_ref.shape[0]):
         total = total + received_ref[s, 0]
     gram, vector = unpack(total)
-    scale = 1.0 / MEMBERS
-    mean_row = jnp.sum(gram, axis=0, keepdims=True) * scale
-    mean_column = jnp.sum(gram, axis=1, keepdims=True) * scale
-    mean_all = jnp.sum(mean_row, axis=1, keepdims=True) * scale
-    vector = vector - mean_row
-    vector = vector - jnp.sum(vector, axis=1, keepdims=True) * scale
     shape = (MEMBERS, MEMBERS)
     identity = jnp.where(iota2(shape, 0) == iota2(shape, 1), 1.0, 0.0)
-    matrix = gram - mean_row - mean_column + mean_all + (MEMBERS - 1.0) * identity
+    matrix = gram + (MEMBERS - 1.0) * identity
     bound = jnp.sum(jnp.sum(jnp.abs(matrix), axis=0, keepdims=True), axis=1, keepdims=True)
     state = matrix / bound
     inverse_root = None
     for sweep in range(ITERS):
         middle = 1.5 * identity - 0.5 * state
-        high, low = halves(middle)
-        right = jnp.concatenate(
-            [jnp.concatenate([high, low], axis=1), jnp.concatenate([low, high], axis=1)], axis=0
-        )
-
-        def times_middle(left):
-            product = dot(jnp.concatenate(halves(left), axis=1), right)
-            return product[:, :MEMBERS] + product[:, MEMBERS:]
-
+        crossed = cross(middle)
         if sweep < ITERS - 1:
-            state = times_middle(times_middle(state))
-        inverse_root = middle if sweep == 0 else times_middle(inverse_root)
+            state = product(product(state, crossed), crossed)
+        inverse_root = middle if sweep == 0 else product(inverse_root, crossed)
     inner = jnp.sum(inverse_root * vector, axis=1, keepdims=True)
     mean_weight = jnp.sum(inverse_root * inner, axis=0, keepdims=True) / bound
     mean_weight = jnp.sum(jnp.where(identity > 0.0, mean_weight, 0.0), axis=1, keepdims=True)
@@ -227,10 +227,10 @@
             axis=0,
         )
         prior_spread = prior_spread_ref[p]
-        product = dot(jnp.concatenate([prior_spread, prior_spread], axis=1), right)
-        post_spread = product[:, :MEMBERS]
+        both = dot(jnp.concatenate([prior_spread, prior_spread], axis=1), right)
+        post_spread = both[:, :MEMBERS]
         spread_ref[p] = post_spread
-        center_ref[p] = prior_center_ref[p] + product[:, MEMBERS:]
+        center_ref[p] = prior_center_ref[p] + both[:, MEMBERS:]
         square = level_sums(jnp.square(post_spread), levels)
         total = square if total is None else total + square
     sums = jnp.concatenate(

time: 76.1 us -> 76.2 us (level)
  no operation moved by 1% of the time
where the time goes in v5:
time: 76.2 us; the launch traced here: 75.9 us
  blocking collectives  61.6 us (81%)
  Pallas kernels  8.51 us (11%)
  starting transfers between devices  5.19 us (7%)
    all_to_all x1, blocking collectives, shards(): sums = lax.all_to_all(sums, 'col', 0, 0, tiled=True)  33.1 us
    all_to_all x1, blocking collectives, shards(): received = lax.all_to_all(sent, 'lag', 0, 0)  17.6 us
    all_to_all x1, blocking collectives, shards(): mixing = lax.all_to_all(solver(received, beside), 'lag', 0, 0)  10.9 us
    ppermute x1, starting transfers between devices, shards(): beside = lax.ppermute(beside, ('lag', 'col'), moves)  5.19 us
    pallas_call x1, Pallas kernels, solver(): pl.pallas_call(solver_kernel, out_shape=jax.ShapeDtypeStruct((received.sh...  3.89 us
    pallas_call x1, Pallas kernels, statistics(): pl.pallas_call(statistics_kernel, out_shape=jax.ShapeDtypeStruct((patches...  1.78 us
  transfers between devices with their start and end apart: 1, of which 1 were waited for; matrix products, arithmetic and copies ran while one was open for 0% of the time, Pallas kernels for 1%

profile of v5, /device:TPU:1, one launch (start us, length us, event | category | flops | bytes accessed | tf_op | source)
XLA Modules:
  0.0 75.9 jit_solution(14151871842828798844)
XLA Ops:
  0.0 0.0 copy-start
  0.0 1.8 %shard_map.55 = f32[8,2,72,128]{3,2,1,0:T(8,128)S(1)} custom-call(s32[1,8]{1,0:T(1,128)} %count_hbm.1, bf16[8,128]{1,0:T(8,128)(2,1)} %bitcast.13, bf16[8,128]{1,0:T(8,128)(2,1)} %bitcast.14, bf16[8,128,128]{2,1,0:T(8,128)(2,1)} %bitcast.12), custom_call_target="tpu_custom_call" | custom-call | tf_op jit(solution)/shard_map/pallas_call | solution.py:123
  1.8 17.6 %all_to_all.21.received_ref = f32[8,2,72,128]{3,2,1,0:T(8,128)S(1)} all-to-all(f32[8,2,72,128]{3,2,1,0:T(8,128)S(1)} %shard_map.55), channel_id=1, replica_groups=mesh['lag'=8,'col'=64] {'lag'}, dimensions={0} | all-to-all | bytes 1179648 | tf_op jit(solution)/shard_map/all_to_all | solution.py:299
  19.4 5.2 %collective-permute-start = (f32[72,128]{1,0:T(8,128)S(1)}, f32[72,128]{1,0:T(8,128)S(1)}, u32[]{:S(2)}, u32[]{:S(2)}) collective-permute-start(f32[72,128]{1,0:T(8,128)S(1)} %slice_reduce_fusion), channel_id=1, source_target_pairs={{0,1},{1,2},{2,3},{3,4},{4,5},{5,6},{6,7},{7,8},{8,9},{9,10},{10,1... | collective-permute-start | bytes 110600 | tf_op jit(solution)/shard_map/ppermute | solution.py:307
  24.6 0.0 copy-done
  24.6 0.5 shard_map.56
  25.0 0.6 collective-permute-done.beside_ref
  25.6 3.9 %shard_map.57 = bf16[8,128,128]{2,1,0:T(8,128)(2,1)S(1)} custom-call(f32[8,2,72,128]{3,2,1,0:T(8,128)S(1)} %all_to_all.21.received_ref, f32[72,128]{1,0:T(8,128)S(1)} %collective-permute-done.beside_ref), custom_call_target="tpu_custom_call" | custom-call | tf_op jit(solution)/shard_map/pallas_call | solution.py:165
  29.5 10.9 %all_to_all.22.mixing_ref = bf16[8,128,128]{2,1,0:T(8,128)(2,1)S(1)} all-to-all(bf16[8,128,128]{2,1,0:T(8,128)(2,1)S(1)} %shard_map.57), channel_id=1, replica_groups=mesh['lag'=8,'col'=64] {'lag'}, dimensions={0} | all-to-all | bytes 524288 | tf_op jit(solution)/shard_map/all_to_all | solution.py:310
  40.4 1.3 %shard_map.58 = (f32[8,384,128]{2,1,0:T(8,128)S(1)}, f32[8,384,128]{2,1,0:T(8,128)S(1)}, f32[64,128]{1,0:T(8,128)S(1)}) custom-call(bf16[8,128,128]{2,1,0:T(8,128)(2,1)S(1)} %all_to_all.22.mixing_ref, bf16[8,384,128]{2,1,0:T(8,128)(2,1)S(1)} %get-tuple-element.19.prior_spread_ref, f32[8,384,128]{2,1,0:T(8,128)S(1)} %get-tuple-element.20.prior_center_ref, ...), custom_call_target="tpu_custom_call" | custom-call | tf_op jit(solution)/shard_map/pallas_call | solution.py:246
  41.7 33.1 %all_to_all.23 = f32[64,1,128]{2,1,0:T(1,128)S(1)} all-to-all(f32[64,1,128]{2,1,0:T(1,128)S(1)} %bitcast.11), channel_id=1, replica_groups=mesh['lag'=8,'col'=64] {'col'}, dimensions={0} | all-to-all | bytes 65536 | tf_op jit(solution)/shard_map/all_to_all | solution.py:312
  74.9 1.1 %shard_map.59 = bf16[8,6,64,128]{3,2,1,0:T(8,128)(2,1)} custom-call(f32[64,128]{1,0:T(8,128)S(1)} %bitcast.10, f32[8,384,128]{2,1,0:T(8,128)S(1)} %get-tuple-element.23.refs_1_, f32[8,384,128]{2,1,0:T(8,128)S(1)} %get-tuple-element.24.refs_2_), custom_call_target="tpu_custom_call" | custom-call | tf_op jit(solution)/shard_map/pallas_call | solution.py:285
  (1 shorter events, 0.0 us)
Async XLA Ops:
  0.0 24.6 %copy-start = (bf16[1,8,6,64,128]{4,3,2,1,0:T(8,128)(2,1)S(1)}, bf16[1,8,6,64,128]{4,3,2,1,0:T(8,128)(2,1)}, u32[]{:S(2)}) copy-start(bf16[1,8,6,64,128]{4,3,2,1,0:T(8,128)(2,1)} %param.5) | copy-start | bytes 2359300
  19.4 6.2 %collective-permute-start = (f32[72,128]{1,0:T(8,128)S(1)}, f32[72,128]{1,0:T(8,128)S(1)}, u32[]{:S(2)}, u32[]{:S(2)}) collective-permute-start(f32[72,128]{1,0:T(8,128)S(1)} %slice_reduce_fusion), channel_id=1, source_target_pairs={{0,1},{1,2},{2,3},{3,4},{4,5},{5,6},{6,7},{7,8},{8,9},{9,10},{10,1... | collective-permute-start | bytes 110600 | tf_op jit(solution)/shard_map/ppermute | solution.py:307

commit v6 on v5

--- a/solution.py
+++ b/solution.py
@@ -12,6 +12,7 @@
 MEMBERS = 128
 HALF = MEMBERS // 2
 PACKED = 72
+PAIR = PACKED + HALF
 
 bf16 = jnp.bfloat16
 f32 = jnp.float32
@@ -30,11 +31,14 @@
     return jnp.dot(left, right, preferred_element_type=f32)
 
 
-def cross(right):
-    high, low = halves(right)
+def crossed_halves(high, low):
     return jnp.concatenate(
         [jnp.concatenate([high, low], axis=1), jnp.concatenate([low, high], axis=1)], axis=0
     )
+
+
+def cross(right):
+    return crossed_halves(*halves(right))
 
 
 def product(left, crossed):
@@ -52,11 +56,9 @@
     return jnp.concatenate([matrix, rest], axis=0)
 
 
-def unpack(packed):
+def unpack(matrix, rest):
     row, lane = iota2((HALF, MEMBERS), 0), iota2((HALF, MEMBERS), 1)
-    matrix = packed[:HALF]
-    diagonal = packed[HALF : HALF + 1]
-    vector = packed[HALF + 1 : HALF + 2]
+    diagonal, vector = rest[0:1], rest[1:2]
     flipped = jnp.transpose(jnp.concatenate([matrix, jnp.zeros_like(matrix)], axis=0))
     upper = jnp.where(lane >= row, matrix, flipped[:HALF])
     corner = jnp.where(lane == row, diagonal, jnp.where(lane < row, matrix, flipped[:HALF]))
@@ -83,32 +85,37 @@
     copies[0].wait()
     for p in range(patches):
         weight = weight_ref[p : p + 1, :].astype(f32)
-        weight = jnp.where(lane < count_ref[:, p : p + 1], weight, 0.0)
+        weight = jnp.sqrt(jnp.where(lane < count_ref[:, p : p + 1], weight, 0.0))
         flipped = jnp.transpose(ensemble_ref[p].astype(f32))
         center = jnp.sum(flipped, axis=0, keepdims=True) * (1.0 / MEMBERS)
         spread = flipped - center
         innovation = value_ref[p : p + 1, :].astype(f32) - center
         innovation = jnp.broadcast_to(innovation, (16, MEMBERS))
-        rows = jnp.concatenate([spread, innovation], axis=0) * weight
+        high, low = halves(jnp.concatenate([spread, innovation], axis=0) * weight)
         both = lax.dot_general(
-            jnp.concatenate(halves(rows), axis=1),
-            cross(spread),
+            jnp.concatenate([high, low], axis=1),
+            crossed_halves(high[:MEMBERS], low[:MEMBERS]),
             (((1,), (1,)), ((), ())),
             preferred_element_type=f32,
         )
         sums = both[:, :MEMBERS] + both[:, MEMBERS:]
         system_ref[p] = pack(sums[:MEMBERS], sums[MEMBERS : MEMBERS + 1])
-    for target in range(-REACH, patches + REACH):
+
+    def tapered(target):
         total = None
         for p in range(patches):
             distance = abs(target - p)
             if distance <= REACH:
                 term = (1.0 - distance / (REACH + 1.0)) * system_ref[p]
                 total = term if total is None else total + term
-        if 0 <= target < patches:
-            out_ref[target, 0] = total
-        else:
-            out_ref[target % patches, 1] = total
+        return total
+
+    for lag in range(patches):
+        own = tapered(lag)
+        beside = tapered(lag + patches if lag < REACH else lag - patches)
+        out_ref[lag, :HALF] = own[:HALF]
+        out_ref[lag, HALF:MEMBERS] = beside[:HALF]
+        out_ref[lag, MEMBERS:] = own[HALF:] + pltpu.roll(beside[HALF:], 2, 0)
 
 
 VMEM = pl.BlockSpec(memory_space=pltpu.VMEM)
@@ -122,7 +129,7 @@
     operands = [pltpu.with_memory_space_constraint(x, pltpu.HBM) for x in operands]
     return pl.pallas_call(
         statistics_kernel,
-        out_shape=jax.ShapeDtypeStruct((patches, 2, PACKED, members), f32),
+        out_shape=jax.ShapeDtypeStruct((patches, PAIR, members), f32),
         in_specs=[HBM] * 4,
         out_specs=VMEM,
         scratch_shapes=[
@@ -138,10 +145,12 @@
 
 
 def solver_kernel(received_ref, beside_ref, out_ref):
-    total = beside_ref[...]
+    matrix = beside_ref[:HALF]
+    rest = pltpu.roll(beside_ref[HALF:], 6, 0)
     for s in range(received_ref.shape[0]):
-        total = total + received_ref[s, 0]
-    gram, vector = unpack(total)
+        matrix = matrix + received_ref[s, :HALF]
+        rest = rest + received_ref[s, MEMBERS:]
+    gram, vector = unpack(matrix, rest)
     shape = (MEMBERS, MEMBERS)
     identity = jnp.where(iota2(shape, 0) == iota2(shape, 1), 1.0, 0.0)
     matrix = gram + (MEMBERS - 1.0) * identity
@@ -297,7 +306,7 @@
     patches, columns = background.shape[1], background.shape[3]
     sent = statistics(obs_count, obs_weight[0], obs_value[0], obs_ensemble[0])
     received = lax.all_to_all(sent, "lag", 0, 0)
-    beside = jnp.sum(received[:, 1], axis=0)
+    beside = jnp.sum(received[:, HALF:], axis=0)
     moves = [
         (i * tiles + c, i * tiles + (c + (1 if i < REACH else -1)) % tiles)
         for i in range(lags)

time: 76.2 us -> 75.9 us (level)
  no operation moved by 1% of the time
where the time goes in v6:
time: 75.9 us; the launch traced here: 75.7 us
  blocking collectives  61.4 us (81%)
  Pallas kernels  8.5 us (11%)
  starting transfers between devices  5.1 us (7%)
    all_to_all x1, blocking collectives, shards(): sums = lax.all_to_all(sums, 'col', 0, 0, tiled=True)  33.2 us
    all_to_all x1, blocking collectives, shards(): received = lax.all_to_all(sent, 'lag', 0, 0)  17.4 us
    all_to_all x1, blocking collectives, shards(): mixing = lax.all_to_all(solver(received, beside), 'lag', 0, 0)  10.8 us
    ppermute x1, starting transfers between devices, shards(): beside = lax.ppermute(beside, ('lag', 'col'), moves)  5.1 us
    pallas_call x1, Pallas kernels, solver(): pl.pallas_call(solver_kernel, out_shape=jax.ShapeDtypeStruct((received.sh...  3.89 us
    pallas_call x1, Pallas kernels, statistics(): pl.pallas_call(statistics_kernel, out_shape=jax.ShapeDtypeStruct((patches...  1.78 us
  transfers between devices with their start and end apart: 1, of which 1 were waited for; matrix products, arithmetic and copies ran while one was open for 0% of the time, Pallas kernels for 1%

profile of v6, /device:TPU:1, one launch (start us, length us, event | category | flops | bytes accessed | tf_op | source)
XLA Modules:
  0.0 75.7 jit_solution(3913933521570888325)
XLA Ops:
  0.0 0.0 copy-start
  0.0 1.8 %shard_map.55 = f32[8,136,128]{2,1,0:T(8,128)S(1)} custom-call(s32[1,8]{1,0:T(1,128)} %count_hbm.1, bf16[8,128]{1,0:T(8,128)(2,1)} %bitcast.13, bf16[8,128]{1,0:T(8,128)(2,1)} %bitcast.14, bf16[8,128,128]{2,1,0:T(8,128)(2,1)} %bitcast.12), custom_call_target="tpu_custom_call" | custom-call | tf_op jit(solution)/shard_map/pallas_call | solution.py:130
  1.8 17.4 %all_to_all.21.received_ref = f32[8,136,128]{2,1,0:T(8,128)S(1)} all-to-all(f32[8,136,128]{2,1,0:T(8,128)S(1)} %shard_map.55), channel_id=1, replica_groups=mesh['lag'=8,'col'=64] {'lag'}, dimensions={0} | all-to-all | bytes 1114112 | tf_op jit(solution)/shard_map/all_to_all | solution.py:308
  19.2 5.1 %collective-permute-start = (f32[72,128]{1,0:T(8,128)S(1)}, f32[72,128]{1,0:T(8,128)S(1)}, u32[]{:S(2)}, u32[]{:S(2)}) collective-permute-start(f32[72,128]{1,0:T(8,128)S(1)} %slice_reduce_fusion), channel_id=1, source_target_pairs={{0,1},{1,2},{2,3},{3,4},{4,5},{5,6},{6,7},{7,8},{8,9},{9,10},{10,1... | collective-permute-start | bytes 110600 | tf_op jit(solution)/shard_map/ppermute | solution.py:316
  24.3 0.0 copy-done
  24.3 0.4 shard_map.56
  24.8 0.6 collective-permute-done.beside_ref
  25.3 3.9 %shard_map.57 = bf16[8,128,128]{2,1,0:T(8,128)(2,1)S(1)} custom-call(f32[8,136,128]{2,1,0:T(8,128)S(1)} %all_to_all.21.received_ref, f32[72,128]{1,0:T(8,128)S(1)} %collective-permute-done.beside_ref), custom_call_target="tpu_custom_call" | custom-call | tf_op jit(solution)/shard_map/pallas_call | solution.py:174
  29.2 10.8 %all_to_all.22.mixing_ref = bf16[8,128,128]{2,1,0:T(8,128)(2,1)S(1)} all-to-all(bf16[8,128,128]{2,1,0:T(8,128)(2,1)S(1)} %shard_map.57), channel_id=1, replica_groups=mesh['lag'=8,'col'=64] {'lag'}, dimensions={0} | all-to-all | bytes 524288 | tf_op jit(solution)/shard_map/all_to_all | solution.py:319
  40.1 1.3 %shard_map.58 = (f32[8,384,128]{2,1,0:T(8,128)S(1)}, f32[8,384,128]{2,1,0:T(8,128)S(1)}, f32[64,128]{1,0:T(8,128)S(1)}) custom-call(bf16[8,128,128]{2,1,0:T(8,128)(2,1)S(1)} %all_to_all.22.mixing_ref, bf16[8,384,128]{2,1,0:T(8,128)(2,1)S(1)} %get-tuple-element.19.prior_spread_ref, f32[8,384,128]{2,1,0:T(8,128)S(1)} %get-tuple-element.20.prior_center_ref, ...), custom_call_target="tpu_custom_call" | custom-call | tf_op jit(solution)/shard_map/pallas_call | solution.py:255
  41.4 33.2 %all_to_all.23 = f32[64,1,128]{2,1,0:T(1,128)S(1)} all-to-all(f32[64,1,128]{2,1,0:T(1,128)S(1)} %bitcast.11), channel_id=1, replica_groups=mesh['lag'=8,'col'=64] {'col'}, dimensions={0} | all-to-all | bytes 65536 | tf_op jit(solution)/shard_map/all_to_all | solution.py:321
  74.6 1.1 %shard_map.59 = bf16[8,6,64,128]{3,2,1,0:T(8,128)(2,1)} custom-call(f32[64,128]{1,0:T(8,128)S(1)} %bitcast.10, f32[8,384,128]{2,1,0:T(8,128)S(1)} %get-tuple-element.23.refs_1_, f32[8,384,128]{2,1,0:T(8,128)S(1)} %get-tuple-element.24.refs_2_), custom_call_target="tpu_custom_call" | custom-call | tf_op jit(solution)/shard_map/pallas_call | solution.py:294
  (1 shorter events, 0.0 us)
Async XLA Ops:
  0.0 24.3 %copy-start = (bf16[1,8,6,64,128]{4,3,2,1,0:T(8,128)(2,1)S(1)}, bf16[1,8,6,64,128]{4,3,2,1,0:T(8,128)(2,1)}, u32[]{:S(2)}) copy-start(bf16[1,8,6,64,128]{4,3,2,1,0:T(8,128)(2,1)} %param.5) | copy-start | bytes 2359300
  19.2 6.1 %collective-permute-start = (f32[72,128]{1,0:T(8,128)S(1)}, f32[72,128]{1,0:T(8,128)S(1)}, u32[]{:S(2)}, u32[]{:S(2)}) collective-permute-start(f32[72,128]{1,0:T(8,128)S(1)} %slice_reduce_fusion), channel_id=1, source_target_pairs={{0,1},{1,2},{2,3},{3,4},{4,5},{5,6},{6,7},{7,8},{8,9},{9,10},{10,1... | collective-permute-start | bytes 110600 | tf_op jit(solution)/shard_map/ppermute | solution.py:316

commit v7 on v6

--- a/solution.py
+++ b/solution.py
@@ -221,22 +221,30 @@
 def apply_kernel(mixing_ref, prior_spread_ref, prior_center_ref, prior_square_ref, spread_ref, center_ref, sums_ref):
     patches = mixing_ref.shape[0]
     levels = prior_square_ref.shape[0]
-    average = jnp.full((MEMBERS, MEMBERS), 1.0 / MEMBERS, bf16)
+    centers = [
+        jnp.broadcast_to(
+            jnp.sum(mixing_ref[p].astype(f32), axis=1, keepdims=True) * (1.0 / MEMBERS),
+            (MEMBERS, MEMBERS),
+        )
+        for p in range(patches)
+    ]
+    rights = []
+    for p in range(patches):
+        spread_high, spread_low = halves(mixing_ref[p].astype(f32) - centers[p])
+        center_high, center_low = halves(centers[p])
+        rights.append(
+            jnp.concatenate(
+                [
+                    jnp.concatenate([spread_high, center_high], axis=1),
+                    jnp.concatenate([spread_low, center_low], axis=1),
+                ],
+                axis=0,
+            )
+        )
     total = None
     for p in range(patches):
-        mixing = mixing_ref[p]
-        mixing_center = dot(mixing, average)
-        spread_high, spread_low = halves(mixing.astype(f32) - mixing_center)
-        center_high, center_low = halves(mixing_center)
-        right = jnp.concatenate(
-            [
-                jnp.concatenate([spread_high, center_high], axis=1),
-                jnp.concatenate([spread_low, center_low], axis=1),
-            ],
-            axis=0,
-        )
         prior_spread = prior_spread_ref[p]
-        both = dot(jnp.concatenate([prior_spread, prior_spread], axis=1), right)
+        both = dot(jnp.concatenate([prior_spread, prior_spread], axis=1), rights[p])
         post_spread = both[:, :MEMBERS]
         spread_ref[p] = post_spread
         center_ref[p] = prior_center_ref[p] + both[:, MEMBERS:]

time: 75.9 us -> 75.4 us (level)
  no operation moved by 1% of the time
where the time goes in v7:
time: 75.4 us; the launch traced here: 75.2 us
  blocking collectives  61.4 us (81%)
  Pallas kernels  8.01 us (11%)
  starting transfers between devices  5.1 us (7%)
    all_to_all x1, blocking collectives, shards(): sums = lax.all_to_all(sums, 'col', 0, 0, tiled=True)  33.2 us
    all_to_all x1, blocking collectives, shards(): received = lax.all_to_all(sent, 'lag', 0, 0)  17.4 us
    all_to_all x1, blocking collectives, shards(): mixing = lax.all_to_all(solver(received, beside), 'lag', 0, 0)  10.8 us
    ppermute x1, starting transfers between devices, shards(): beside = lax.ppermute(beside, ('lag', 'col'), moves)  5.1 us
    pallas_call x1, Pallas kernels, solver(): pl.pallas_call(solver_kernel, out_shape=jax.ShapeDtypeStruct((received.sh...  3.89 us
    pallas_call x1, Pallas kernels, statistics(): pl.pallas_call(statistics_kernel, out_shape=jax.ShapeDtypeStruct((patches...  1.78 us
  transfers between devices with their start and end apart: 1, of which 1 were waited for; matrix products, arithmetic and copies ran while one was open for 0% of the time, Pallas kernels for 1%

profile of v7, /device:TPU:1, one launch (start us, length us, event | category | flops | bytes accessed | tf_op | source)
XLA Modules:
  0.0 75.2 jit_solution(8909583730549485547)
XLA Ops:
  0.0 0.0 copy-start
  0.0 1.8 %shard_map.55 = f32[8,136,128]{2,1,0:T(8,128)S(1)} custom-call(s32[1,8]{1,0:T(1,128)} %count_hbm.1, bf16[8,128]{1,0:T(8,128)(2,1)} %bitcast.13, bf16[8,128]{1,0:T(8,128)(2,1)} %bitcast.14, bf16[8,128,128]{2,1,0:T(8,128)(2,1)} %bitcast.12), custom_call_target="tpu_custom_call" | custom-call | tf_op jit(solution)/shard_map/pallas_call | solution.py:130
  1.8 17.4 %all_to_all.21.received_ref = f32[8,136,128]{2,1,0:T(8,128)S(1)} all-to-all(f32[8,136,128]{2,1,0:T(8,128)S(1)} %shard_map.55), channel_id=1, replica_groups=mesh['lag'=8,'col'=64] {'lag'}, dimensions={0} | all-to-all | bytes 1114112 | tf_op jit(solution)/shard_map/all_to_all | solution.py:316
  19.2 5.1 %collective-permute-start = (f32[72,128]{1,0:T(8,128)S(1)}, f32[72,128]{1,0:T(8,128)S(1)}, u32[]{:S(2)}, u32[]{:S(2)}) collective-permute-start(f32[72,128]{1,0:T(8,128)S(1)} %slice_reduce_fusion), channel_id=1, source_target_pairs={{0,1},{1,2},{2,3},{3,4},{4,5},{5,6},{6,7},{7,8},{8,9},{9,10},{10,1... | collective-permute-start | bytes 110600 | tf_op jit(solution)/shard_map/ppermute | solution.py:324
  24.3 0.0 copy-done
  24.3 0.4 shard_map.56
  24.8 0.6 collective-permute-done.beside_ref
  25.3 3.9 %shard_map.57 = bf16[8,128,128]{2,1,0:T(8,128)(2,1)S(1)} custom-call(f32[8,136,128]{2,1,0:T(8,128)S(1)} %all_to_all.21.received_ref, f32[72,128]{1,0:T(8,128)S(1)} %collective-permute-done.beside_ref), custom_call_target="tpu_custom_call" | custom-call | tf_op jit(solution)/shard_map/pallas_call | solution.py:174
  29.2 10.8 %all_to_all.22.mixing_ref = bf16[8,128,128]{2,1,0:T(8,128)(2,1)S(1)} all-to-all(bf16[8,128,128]{2,1,0:T(8,128)(2,1)S(1)} %shard_map.57), channel_id=1, replica_groups=mesh['lag'=8,'col'=64] {'lag'}, dimensions={0} | all-to-all | bytes 524288 | tf_op jit(solution)/shard_map/all_to_all | solution.py:327
  40.1 0.8 %shard_map.58 = (f32[8,384,128]{2,1,0:T(8,128)S(1)}, f32[8,384,128]{2,1,0:T(8,128)S(1)}, f32[64,128]{1,0:T(8,128)S(1)}) custom-call(bf16[8,128,128]{2,1,0:T(8,128)(2,1)S(1)} %all_to_all.22.mixing_ref, bf16[8,384,128]{2,1,0:T(8,128)(2,1)S(1)} %get-tuple-element.19.prior_spread_ref, f32[8,384,128]{2,1,0:T(8,128)S(1)} %get-tuple-element.20.prior_center_ref, ...), custom_call_target="tpu_custom_call" | custom-call | tf_op jit(solution)/shard_map/pallas_call | solution.py:263
  40.9 33.2 %all_to_all.23 = f32[64,1,128]{2,1,0:T(1,128)S(1)} all-to-all(f32[64,1,128]{2,1,0:T(1,128)S(1)} %bitcast.11), channel_id=1, replica_groups=mesh['lag'=8,'col'=64] {'col'}, dimensions={0} | all-to-all | bytes 65536 | tf_op jit(solution)/shard_map/all_to_all | solution.py:329
  74.1 1.1 %shard_map.59 = bf16[8,6,64,128]{3,2,1,0:T(8,128)(2,1)} custom-call(f32[64,128]{1,0:T(8,128)S(1)} %bitcast.10, f32[8,384,128]{2,1,0:T(8,128)S(1)} %get-tuple-element.23.refs_1_, f32[8,384,128]{2,1,0:T(8,128)S(1)} %get-tuple-element.24.refs_2_), custom_call_target="tpu_custom_call" | custom-call | tf_op jit(solution)/shard_map/pallas_call | solution.py:302
  (1 shorter events, 0.0 us)
Async XLA Ops:
  0.0 24.3 %copy-start = (bf16[1,8,6,64,128]{4,3,2,1,0:T(8,128)(2,1)S(1)}, bf16[1,8,6,64,128]{4,3,2,1,0:T(8,128)(2,1)}, u32[]{:S(2)}) copy-start(bf16[1,8,6,64,128]{4,3,2,1,0:T(8,128)(2,1)} %param.5) | copy-start | bytes 2359300
  19.2 6.1 %collective-permute-start = (f32[72,128]{1,0:T(8,128)S(1)}, f32[72,128]{1,0:T(8,128)S(1)}, u32[]{:S(2)}, u32[]{:S(2)}) collective-permute-start(f32[72,128]{1,0:T(8,128)S(1)} %slice_reduce_fusion), channel_id=1, source_target_pairs={{0,1},{1,2},{2,3},{3,4},{4,5},{5,6},{6,7},{7,8},{8,9},{9,10},{10,1... | collective-permute-start | bytes 110600 | tf_op jit(solution)/shard_map/ppermute | solution.py:324
